TPU v7x, 32 devices: a whole 2x2x4 slice. The times are simulated.
32 devices in a mesh: groups: 2 (over x), context: 16 (over z, y, core).
Axes of the slice: x: 2, y: 2, z: 4, core: 2. Of those that a mesh axis runs over, the one named last changes fastest.
Arguments:
- queries: bfloat16 [4096, 16, 128], P(('groups', 'context')), parts along dimension 0, may hold values from -24 to 24
- keys: bfloat16 [4096, 8, 128], P(('groups', 'context')), parts along dimension 0, may hold values from -24 to 24
- values: bfloat16 [4096, 8, 128], P(('groups', 'context')), parts along dimension 0, may hold values from -6 to 6
- grad_out: bfloat16 [4096, 16, 128], P(('groups', 'context')), parts along dimension 0, may hold values from -24 to 24
- readout: float32 [16, 128], replicated, may hold values from -4 to 4
- segments: int32 [4096], P(('groups', 'context')), parts along dimension 0, may hold values from 0 to 3, never falling along the last dimension, each value on 1 to 1024 neighbouring positions
- loss_mask: int32 [4096], P(('groups', 'context')), parts along dimension 0, may hold values from 0 to 1, as said below
- labels: int32 [4096], P(('groups', 'context')), parts along dimension 0, may hold values 0 or 1
Outputs:
- grad_queries: bfloat16 [4096, 16, 128], P(('groups', 'context')), parts along dimension 0
- grad_keys: bfloat16 [4096, 8, 128], P(('groups', 'context')), parts along dimension 0
- grad_values: bfloat16 [4096, 8, 128], P(('groups', 'context')), parts along dimension 0
There are 2 independent parts, one for each index of `groups`. A program takes and returns all parts, laid end to end along the dimension named above; an argument that names none is the same for every part. Nothing has to cross between parts.
Inputs may be any that keep to these rules, and one draw needn't show every extreme that they name: `loss_mask`: every entry of the first 128 positions is 0.
All inputs are finite; a program needn't handle non-finite values. No bound on the sum of `labels` on one device may be relied on, other than what follows from the above.
Results may differ from a plain program's by a relative error of at most 0.025.
Values may be sent and summed in bfloat16 or wider, within the bound.
A program may use at most 128 MiB of HBM per device.

v0:
```python
import jax
import jax.numpy as jnp
from jax import lax
from jax.sharding import PartitionSpec as P

WINDOW = 1024


SCALE = 168.0 ** (-0.5)
NEGATIVE = -1e30


def from_behind(block, axis, distance):
    devices = range(lax.axis_size(axis))
    route = [(i - distance, i) for i in devices if i - distance in devices]
    return lax.ppermute(block, axis, route)


def masked_scores(query_group, key_part, mask):
    scores = (
        jnp.einsum("qgrd,kgd->grqk", query_group, key_part, preferred_element_type=jnp.float32)
        * SCALE
    )
    return jnp.where(mask, scores, NEGATIVE)


def normalize(scores, mask):
    row_max = jnp.max(scores, axis=-1, keepdims=True)
    row_total = jnp.sum(jnp.where(mask, jnp.exp(scores - row_max), 0.0), axis=-1, keepdims=True)
    log_total = row_max + jnp.log(row_total)
    return jnp.where(mask, jnp.exp(scores - log_total), 0.0)


def local(queries, keys, values, grad_out, readout, segments, loss_mask, labels):
    row_count = queries.shape[0]
    head_count = queries.shape[1]
    kv_count = keys.shape[1]
    head_dim = queries.shape[2]
    ratio = head_count // kv_count
    kv_group = 2
    halo_depth = WINDOW // row_count
    my_index = lax.axis_index("context")
    seg_wire = segments.astype(jnp.bfloat16)
    fetched = [
        from_behind((keys, values, seg_wire), "context", offset)
        for offset in range(1, halo_depth + 1)
    ]
    ordered = fetched[::-1]
    key_window = jnp.concatenate([piece[0] for piece in ordered] + [keys], axis=0)
    value_window = jnp.concatenate([piece[1] for piece in ordered] + [values], axis=0)
    seg_window = jnp.concatenate(
        [piece[2].astype(jnp.int32) for piece in ordered] + [segments], axis=0
    )
    query_pos = my_index * row_count + jnp.arange(row_count, dtype=jnp.int32)
    key_pos = (my_index - halo_depth) * row_count + jnp.arange(
        row_count * (halo_depth + 1), dtype=jnp.int32
    )
    distance = query_pos[:, None] - key_pos[None, :]
    allowed = (
        (distance >= 0)
        & (distance < WINDOW)
        & (key_pos[None, :] >= 0)
        & (segments[:, None] == seg_window[None, :])
    )
    mask = allowed[None, None]
    spans = [
        (slice(start, start + kv_group), slice(start * ratio, (start + kv_group) * ratio))
        for start in range(0, kv_count, kv_group)
    ]

    def split_heads(array):
        return array.reshape(row_count, kv_group, ratio, head_dim)

    probs = []
    outputs = []
    for kv_span, q_span in spans:
        prob = normalize(
            masked_scores(split_heads(queries[:, q_span]), key_window[:, kv_span], mask), mask
        )
        prob_low = prob.astype(jnp.bfloat16)
        out = jnp.einsum(
            "grqk,kgd->qgrd", prob_low, value_window[:, kv_span], preferred_element_type=jnp.float32
        )
        outputs.append(out.reshape(row_count, kv_group * ratio, head_dim))
        probs.append((prob, prob_low))
    attn_out = jnp.concatenate(outputs, axis=1)
    reward = jnp.sum(attn_out * readout[None], axis=(1, 2))
    live_rows = loss_mask.astype(jnp.float32)
    probe_grad = live_rows * (jax.nn.sigmoid(reward) - labels.astype(jnp.float32))
    grad_attn = (
        live_rows[:, None, None] * grad_out.astype(jnp.float32)
        + probe_grad[:, None, None] * readout[None]
    ).astype(jnp.bfloat16)
    delta = jnp.sum(grad_attn.astype(jnp.float32) * attn_out, axis=-1)
    query_parts = []
    key_parts = []
    value_parts = []
    for (kv_span, q_span), (prob, prob_low) in zip(spans, probs):
        grad_part = split_heads(grad_attn[:, q_span])
        query_group = split_heads(queries[:, q_span])
        grad_prob = jnp.einsum(
            "qgrd,kgd->grqk",
            grad_part,
            value_window[:, kv_span],
            preferred_element_type=jnp.float32,
        )
        delta_part = delta[:, q_span].reshape(row_count, kv_group, ratio)
        grad_score = (prob * (grad_prob - jnp.transpose(delta_part, (1, 2, 0))[..., None])).astype(
            jnp.bfloat16
        )
        query_grad = (
            jnp.einsum(
                "grqk,kgd->qgrd",
                grad_score,
                key_window[:, kv_span],
                preferred_element_type=jnp.float32,
            )
            * SCALE
        )
        query_parts.append(query_grad.reshape(row_count, kv_group * ratio, head_dim))
        key_parts.append(
            jnp.einsum(
                "grqk,qgrd->kgd", grad_score, query_group, preferred_element_type=jnp.float32
            )
            * SCALE
        )
        value_parts.append(
            jnp.einsum("grqk,qgrd->kgd", prob_low, grad_part, preferred_element_type=jnp.float32)
        )
    grad_queries = jnp.concatenate(query_parts, axis=1).astype(jnp.bfloat16)
    grad_queries, key_grads, value_grads = (
        grad_queries,
        jnp.concatenate(key_parts, axis=1),
        jnp.concatenate(value_parts, axis=1),
    )

    def block_of(array, offset):
        start = (halo_depth - offset) * row_count
        return array[start : start + row_count]

    key_total = block_of(key_grads, 0)
    value_total = block_of(value_grads, 0)
    for offset in range(1, halo_depth + 1):
        got_keys, got_values = from_behind(
            (block_of(key_grads, offset), block_of(value_grads, offset)), "context", -offset
        )
        key_total = key_total + got_keys
        value_total = value_total + got_values
    return (grad_queries, key_total.astype(jnp.bfloat16), value_total.astype(jnp.bfloat16))


def solution(mesh):
    in_specs = (
        P(("groups", "context"), None, None),
        P(("groups", "context"), None, None),
        P(("groups", "context"), None, None),
        P(("groups", "context"), None, None),
        P(),
        P(("groups", "context")),
        P(("groups", "context")),
        P(("groups", "context")),
    )
    out_specs = (
        P(("groups", "context"), None, None),
        P(("groups", "context"), None, None),
        P(("groups", "context"), None, None),
    )
    return jax.shard_map(local, mesh=mesh, in_specs=in_specs, out_specs=out_specs, check_vma=False)
```

profile of v0, /device:TPU:12, one launch (start us, length us, event | category | flops | bytes accessed | tf_op | source)
XLA Modules:
  0.0 461.2 jit_solution(8193998955481126626)
XLA Ops:
  3.3 3.4 collective-permute-start.14
  6.7 4.4 collective-permute-start.13
  22.3 5.6 %collective-permute-start.10 = (bf16[128]{0:T(256)(128)(2,1)S(1)}, bf16[128]{0:T(256)(128)(2,1)S(1)}, u32[]{:S(2)}, u32[]{:S(2)}) collective-permute-start(bf16[128]{0:T(256)(128)(2,1)S(1)} %convert_element_type.73), channel_id=1, source_target_pairs={{0,6},{1,7},{2,8},{3,9},{4,10},{5,11},{6,12},{7,13},{8,14},{9,15},... | collective-permute-start | bytes 776 | tf_op jit(solution)/shard_map/ppermute | solution.py:16
  29.2 3.1 collective-permute-start.11
  32.3 2.7 collective-permute-done.11
  34.9 2.9 collective-permute-start.7
  37.9 6.5 %collective-permute-start.6 = (bf16[128,8,128]{2,0,1:T(8,128)(2,1)S(1)}, bf16[128,8,128]{2,0,1:T(8,128)(2,1)S(1)}, u32[]{:S(2)}, u32[]{:S(2)}) collective-permute-start(bf16[128,8,128]{2,0,1:T(8,128)(2,1)S(1)} %copy.135), channel_id=1, source_target_pairs={{0,2},{1,3},{2,4},{3,5},{4,6},{5,7},{6,8},{7,9},{8,10},{9,11},{10,... | collective-permute-start | bytes 786440 | tf_op jit(solution)/shard_map/ppermute | solution.py:16
  50.1 37.5 %collective-permute-done.16 = bf16[128,8,128]{0,2,1:T(8,128)(2,1)S(1)} collective-permute-done((bf16[128,8,128]{0,2,1:T(8,128)(2,1)S(1)}, bf16[128,8,128]{0,2,1:T(8,128)(2,1)S(1)}, u32[]{:S(2)}, u32[]{:S(2)}) %collective-permute-start.16) | collective-permute-done | bytes 262176 | tf_op jit(solution)/shard_map/ppermute | solution.py:16
  89.6 5.6 %collective-permute-start.20 = (bf16[128,8,128]{0,2,1:T(8,128)(2,1)S(1)}, bf16[128,8,128]{0,2,1:T(8,128)(2,1)S(1)}, u32[]{:S(2)}, u32[]{:S(2)}) collective-permute-start(bf16[128,8,128]{0,2,1:T(8,128)(2,1)S(1)} %copy.145), channel_id=1, source_target_pairs={{0,4},{1,5},{2,6},{3,7},{4,8},{5,9},{6,10},{7,11},{8,12},{9,13},{1... | collective-permute-start | bytes 786440 | tf_op jit(solution)/shard_map/ppermute | solution.py:16
  95.2 2.8 collective-permute-start.21
  100.2 2.5 collective-permute-done.20
  104.6 2.9 collective-permute-done.21
  109.8 3.3 collective-permute-done.22
  114.5 7.9 %collective-permute-start.1 = (bf16[128,8,128]{2,0,1:T(8,128)(2,1)S(1)}, bf16[128,8,128]{2,0,1:T(8,128)(2,1)S(1)}, u32[]{:S(2)}, u32[]{:S(2)}) collective-permute-start(bf16[128,8,128]{2,0,1:T(8,128)(2,1)S(1)} %copy.135), channel_id=1, source_target_pairs={{0,7},{1,8},{2,9},{3,10},{4,11},{5,12},{6,13},{7,14},{8,15},{16,23... | collective-permute-start | bytes 786440 | tf_op jit(solution)/shard_map/ppermute | solution.py:16
  122.5 18.7 %collective-permute-done = bf16[128,8,128]{2,0,1:T(8,128)(2,1)S(1)} collective-permute-done((bf16[128,8,128]{2,0,1:T(8,128)(2,1)S(1)}, bf16[128,8,128]{2,0,1:T(8,128)(2,1)S(1)}, u32[]{:S(2)}, u32[]{:S(2)}) %collective-permute-start) | collective-permute-done | bytes 262176 | tf_op jit(solution)/shard_map/ppermute | solution.py:16
  143.2 6.5 %collective-permute-done.1 = bf16[128,8,128]{2,0,1:T(8,128)(2,1)S(1)} collective-permute-done((bf16[128,8,128]{2,0,1:T(8,128)(2,1)S(1)}, bf16[128,8,128]{2,0,1:T(8,128)(2,1)S(1)}, u32[]{:S(2)}, u32[]{:S(2)}) %collective-permute-start.1) | collective-permute-done | bytes 262176 | tf_op jit(solution)/shard_map/ppermute | solution.py:16
  149.7 6.6 %collective-permute-start.4 = (bf16[128,8,128]{2,0,1:T(8,128)(2,1)S(1)}, bf16[128,8,128]{2,0,1:T(8,128)(2,1)S(1)}, u32[]{:S(2)}, u32[]{:S(2)}) collective-permute-start(bf16[128,8,128]{2,0,1:T(8,128)(2,1)S(1)} %copy.135), channel_id=1, source_target_pairs={{0,4},{1,5},{2,6},{3,7},{4,8},{5,9},{6,10},{7,11},{8,12},{9,13},{1... | collective-permute-start | bytes 786440 | tf_op jit(solution)/shard_map/ppermute | solution.py:16
  158.6 4.5 collective-permute-done.4
  163.1 5.6 %collective-permute-done.5 = bf16[128,8,128]{2,0,1:T(8,128)(2,1)S(1)} collective-permute-done((bf16[128,8,128]{2,0,1:T(8,128)(2,1)S(1)}, bf16[128,8,128]{2,0,1:T(8,128)(2,1)S(1)}, u32[]{:S(2)}, u32[]{:S(2)}) %collective-permute-start.5) | collective-permute-done | bytes 262176 | tf_op jit(solution)/shard_map/ppermute | solution.py:16
  173.6 2.4 fusion.57
  176.8 2.4 fusion.56
  189.4 2.4 convolution_bitcast_fusion.4
  217.8 10.1 %collective-permute-done.31 = f32[128,8,128]{2,0,1:T(8,128)S(1)} collective-permute-done((f32[128,8,128]{2,0,1:T(8,128)}, f32[128,8,128]{2,0,1:T(8,128)S(1)}, u32[]{:S(2)}, u32[]{:S(2)}) %collective-permute-start.31) | collective-permute-done | bytes 524320 | tf_op jit(solution)/shard_map/ppermute | solution.py:16
  227.9 16.4 %collective-permute-start.26 = (f32[128,8,128]{2,0,1:T(8,128)S(1)}, f32[128,8,128]{2,0,1:T(8,128)S(1)}, u32[]{:S(2)}, u32[]{:S(2)}) collective-permute-start(f32[128,8,128]{2,0,1:T(8,128)S(1)} %get-tuple-element.32), channel_id=1, source_target_pairs={{3,0},{4,1},{5,2},{6,3},{7,4},{8,5},{9,6},{10,7},{11,8},{12,9},{13... | collective-permute-start | bytes 1572872 | tf_op jit(solution)/shard_map/ppermute | solution.py:16
  244.3 24.4 %collective-permute-start.25 = (f32[128,8,128]{2,0,1:T(8,128)S(1)}, f32[128,8,128]{2,0,1:T(8,128)S(1)}, u32[]{:S(2)}, u32[]{:S(2)}) collective-permute-start(f32[128,8,128]{2,0,1:T(8,128)S(1)} %get-tuple-element.33), channel_id=1, source_target_pairs={{2,0},{3,1},{4,2},{5,3},{6,4},{7,5},{8,6},{9,7},{10,8},{11,9},{12,... | collective-permute-start | bytes 1572872 | tf_op jit(solution)/shard_map/ppermute | solution.py:16
  268.7 10.9 %collective-permute-start.32 = (f32[128,8,128]{0,2,1:T(8,128)S(1)}, f32[128,8,128]{0,2,1:T(8,128)S(1)}, u32[]{:S(2)}, u32[]{:S(2)}) collective-permute-start(f32[128,8,128]{0,2,1:T(8,128)S(1)} %get-tuple-element.18), channel_id=1, source_target_pairs={{1,0},{2,1},{3,2},{4,3},{5,4},{6,5},{7,6},{8,7},{9,8},{10,9},{11,1... | collective-permute-start | bytes 1572872 | tf_op jit(solution)/shard_map/ppermute | solution.py:16
  280.9 16.5 %collective-permute-done.27 = f32[128,8,128]{2,0,1:T(8,128)S(1)} collective-permute-done((f32[128,8,128]{2,0,1:T(8,128)S(1)}, f32[128,8,128]{2,0,1:T(8,128)S(1)}, u32[]{:S(2)}, u32[]{:S(2)}) %collective-permute-start.27) | collective-permute-done | bytes 524320 | tf_op jit(solution)/shard_map/ppermute | solution.py:16
  300.1 47.3 %collective-permute-done.26 = f32[128,8,128]{2,0,1:T(8,128)S(1)} collective-permute-done((f32[128,8,128]{2,0,1:T(8,128)S(1)}, f32[128,8,128]{2,0,1:T(8,128)S(1)}, u32[]{:S(2)}, u32[]{:S(2)}) %collective-permute-start.26) | collective-permute-done | bytes 524320 | tf_op jit(solution)/shard_map/ppermute | solution.py:16
  349.3 28.2 %collective-permute-done.25 = f32[128,8,128]{2,0,1:T(8,128)S(1)} collective-permute-done((f32[128,8,128]{2,0,1:T(8,128)S(1)}, f32[128,8,128]{2,0,1:T(8,128)S(1)}, u32[]{:S(2)}, u32[]{:S(2)}) %collective-permute-start.25) | collective-permute-done | bytes 524320 | tf_op jit(solution)/shard_map/ppermute | solution.py:16
  383.4 3.0 collective-permute-start.33
  395.5 42.0 %collective-permute-done.34 = f32[128,8,128]{0,2,1:T(8,128)} collective-permute-done((f32[128,8,128]{0,2,1:T(8,128)}, f32[128,8,128]{0,2,1:T(8,128)}, u32[]{:S(2)}, u32[]{:S(2)}) %collective-permute-start.34) | collective-permute-done | bytes 524320 | tf_op jit(solution)/shard_map/ppermute | solution.py:16
  437.5 20.7 %collective-permute-done.33 = f32[128,8,128]{0,2,1:T(8,128)} collective-permute-done((f32[128,8,128]{0,2,1:T(8,128)S(1)}, f32[128,8,128]{0,2,1:T(8,128)}, u32[]{:S(2)}, u32[]{:S(2)}) %collective-permute-start.33) | collective-permute-done | bytes 524320 | tf_op jit(solution)/shard_map/ppermute | solution.py:16
  (222 shorter events, 99.6 us)
Async XLA Ops:
  1.4 46.3 %collective-permute-start.15 = (bf16[128]{0:T(256)(128)(2,1)S(1)}, bf16[128]{0:T(256)(128)(2,1)S(1)}, u32[]{:S(2)}, u32[]{:S(2)}) collective-permute-start(bf16[128]{0:T(256)(128)(2,1)S(1)} %convert_element_type.73), channel_id=1, source_target_pairs={{0,1},{1,2},{2,3},{3,4},{4,5},{5,6},{6,7},{7,8},{8,9},{9,10},{10,1... | collective-permute-start | bytes 776 | tf_op jit(solution)/shard_map/ppermute | solution.py:16
  3.3 43.1 %collective-permute-start.14 = (bf16[128]{0:T(256)(128)(2,1)S(1)}, bf16[128]{0:T(256)(128)(2,1)S(1)}, u32[]{:S(2)}, u32[]{:S(2)}) collective-permute-start(bf16[128]{0:T(256)(128)(2,1)S(1)} %convert_element_type.73), channel_id=1, source_target_pairs={{0,2},{1,3},{2,4},{3,5},{4,6},{5,7},{6,8},{7,9},{8,10},{9,11},{10,... | collective-permute-start | bytes 776 | tf_op jit(solution)/shard_map/ppermute | solution.py:16
  6.7 37.7 %collective-permute-start.13 = (bf16[128]{0:T(256)(128)(2,1)S(1)}, bf16[128]{0:T(256)(128)(2,1)S(1)}, u32[]{:S(2)}, u32[]{:S(2)}) collective-permute-start(bf16[128]{0:T(256)(128)(2,1)S(1)} %convert_element_type.73), channel_id=1, source_target_pairs={{0,3},{1,4},{2,5},{3,6},{4,7},{5,8},{6,9},{7,10},{8,11},{9,12},{10... | collective-permute-start | bytes 776 | tf_op jit(solution)/shard_map/ppermute | solution.py:16
  11.1 26.8 %collective-permute-start.12 = (bf16[128]{0:T(256)(128)(2,1)S(1)}, bf16[128]{0:T(256)(128)(2,1)S(1)}, u32[]{:S(2)}, u32[]{:S(2)}) collective-permute-start(bf16[128]{0:T(256)(128)(2,1)S(1)} %convert_element_type.73), channel_id=1, source_target_pairs={{0,4},{1,5},{2,6},{3,7},{4,8},{5,9},{6,10},{7,11},{8,12},{9,13},{1... | collective-permute-start | bytes 776 | tf_op jit(solution)/shard_map/ppermute | solution.py:16
  34.9 133.8 %collective-permute-start.7 = (bf16[128,8,128]{2,0,1:T(8,128)(2,1)S(1)}, bf16[128,8,128]{2,0,1:T(8,128)(2,1)S(1)}, u32[]{:S(2)}, u32[]{:S(2)}) collective-permute-start(bf16[128,8,128]{2,0,1:T(8,128)(2,1)S(1)} %copy.135), channel_id=1, source_target_pairs={{0,1},{1,2},{2,3},{3,4},{4,5},{5,6},{6,7},{7,8},{8,9},{9,10},{10,1... | collective-permute-start | bytes 786440 | tf_op jit(solution)/shard_map/ppermute | solution.py:16
  37.9 130.8 %collective-permute-start.6 = (bf16[128,8,128]{2,0,1:T(8,128)(2,1)S(1)}, bf16[128,8,128]{2,0,1:T(8,128)(2,1)S(1)}, u32[]{:S(2)}, u32[]{:S(2)}) collective-permute-start(bf16[128,8,128]{2,0,1:T(8,128)(2,1)S(1)} %copy.135), channel_id=1, source_target_pairs={{0,2},{1,3},{2,4},{3,5},{4,6},{5,7},{6,8},{7,9},{8,10},{9,11},{10,... | collective-permute-start | bytes 786440 | tf_op jit(solution)/shard_map/ppermute | solution.py:16
  44.4 50.9 %collective-permute-start.18 = (bf16[128,8,128]{0,2,1:T(8,128)(2,1)S(1)}, bf16[128,8,128]{0,2,1:T(8,128)(2,1)S(1)}, u32[]{:S(2)}, u32[]{:S(2)}) collective-permute-start(bf16[128,8,128]{0,2,1:T(8,128)(2,1)S(1)} %copy.145), channel_id=1, source_target_pairs={{0,6},{1,7},{2,8},{3,9},{4,10},{5,11},{6,12},{7,13},{8,14},{9,15},... | collective-permute-start | bytes 786440 | tf_op jit(solution)/shard_map/ppermute | solution.py:16
  46.3 43.2 %collective-permute-start.17 = (bf16[128,8,128]{0,2,1:T(8,128)(2,1)S(1)}, bf16[128,8,128]{0,2,1:T(8,128)(2,1)S(1)}, u32[]{:S(2)}, u32[]{:S(2)}) collective-permute-start(bf16[128,8,128]{0,2,1:T(8,128)(2,1)S(1)} %copy.145), channel_id=1, source_target_pairs={{0,7},{1,8},{2,9},{3,10},{4,11},{5,12},{6,13},{7,14},{8,15},{16,23... | collective-permute-start | bytes 786440 | tf_op jit(solution)/shard_map/ppermute | solution.py:16
  47.7 39.9 %collective-permute-start.16 = (bf16[128,8,128]{0,2,1:T(8,128)(2,1)S(1)}, bf16[128,8,128]{0,2,1:T(8,128)(2,1)S(1)}, u32[]{:S(2)}, u32[]{:S(2)}) collective-permute-start(bf16[128,8,128]{0,2,1:T(8,128)(2,1)S(1)} %copy.145), channel_id=1, source_target_pairs={{0,8},{1,9},{2,10},{3,11},{4,12},{5,13},{6,14},{7,15},{16,24},{17,... | collective-permute-start | bytes 786440 | tf_op jit(solution)/shard_map/ppermute | solution.py:16
  89.6 13.1 %collective-permute-start.20 = (bf16[128,8,128]{0,2,1:T(8,128)(2,1)S(1)}, bf16[128,8,128]{0,2,1:T(8,128)(2,1)S(1)}, u32[]{:S(2)}, u32[]{:S(2)}) collective-permute-start(bf16[128,8,128]{0,2,1:T(8,128)(2,1)S(1)} %copy.145), channel_id=1, source_target_pairs={{0,4},{1,5},{2,6},{3,7},{4,8},{5,9},{6,10},{7,11},{8,12},{9,13},{1... | collective-permute-start | bytes 786440 | tf_op jit(solution)/shard_map/ppermute | solution.py:16
  98.2 14.9 %collective-permute-start.22 = (bf16[128,8,128]{0,2,1:T(8,128)(2,1)S(1)}, bf16[128,8,128]{0,2,1:T(8,128)(2,1)S(1)}, u32[]{:S(2)}, u32[]{:S(2)}) collective-permute-start(bf16[128,8,128]{0,2,1:T(8,128)(2,1)S(1)} %copy.145), channel_id=1, source_target_pairs={{0,2},{1,3},{2,4},{3,5},{4,6},{5,7},{6,8},{7,9},{8,10},{9,11},{10,... | collective-permute-start | bytes 786440 | tf_op jit(solution)/shard_map/ppermute | solution.py:16
  107.5 48.8 %collective-permute-start.2 = (bf16[128,8,128]{2,0,1:T(8,128)(2,1)S(1)}, bf16[128,8,128]{2,0,1:T(8,128)(2,1)S(1)}, u32[]{:S(2)}, u32[]{:S(2)}) collective-permute-start(bf16[128,8,128]{2,0,1:T(8,128)(2,1)S(1)} %copy.135), channel_id=1, source_target_pairs={{0,6},{1,7},{2,8},{3,9},{4,10},{5,11},{6,12},{7,13},{8,14},{9,15},... | collective-permute-start | bytes 786440 | tf_op jit(solution)/shard_map/ppermute | solution.py:16
  113.1 28.1 %collective-permute-start = (bf16[128,8,128]{2,0,1:T(8,128)(2,1)S(1)}, bf16[128,8,128]{2,0,1:T(8,128)(2,1)S(1)}, u32[]{:S(2)}, u32[]{:S(2)}) collective-permute-start(bf16[128,8,128]{2,0,1:T(8,128)(2,1)S(1)} %copy.135), channel_id=1, source_target_pairs={{0,8},{1,9},{2,10},{3,11},{4,12},{5,13},{6,14},{7,15},{16,24},{17,... | collective-permute-start | bytes 786440 | tf_op jit(solution)/shard_map/ppermute | solution.py:16
  114.5 35.2 %collective-permute-start.1 = (bf16[128,8,128]{2,0,1:T(8,128)(2,1)S(1)}, bf16[128,8,128]{2,0,1:T(8,128)(2,1)S(1)}, u32[]{:S(2)}, u32[]{:S(2)}) collective-permute-start(bf16[128,8,128]{2,0,1:T(8,128)(2,1)S(1)} %copy.135), channel_id=1, source_target_pairs={{0,7},{1,8},{2,9},{3,10},{4,11},{5,12},{6,13},{7,14},{8,15},{16,23... | collective-permute-start | bytes 786440 | tf_op jit(solution)/shard_map/ppermute | solution.py:16
  141.2 17.3 %collective-permute-start.3 = (bf16[128,8,128]{2,0,1:T(8,128)(2,1)S(1)}, bf16[128,8,128]{2,0,1:T(8,128)(2,1)S(1)}, u32[]{:S(2)}, u32[]{:S(2)}) collective-permute-start(bf16[128,8,128]{2,0,1:T(8,128)(2,1)S(1)} %copy.135), channel_id=1, source_target_pairs={{0,5},{1,6},{2,7},{3,8},{4,9},{5,10},{6,11},{7,12},{8,13},{9,14},{... | collective-permute-start | bytes 786440 | tf_op jit(solution)/shard_map/ppermute | solution.py:16
  149.7 13.4 %collective-permute-start.4 = (bf16[128,8,128]{2,0,1:T(8,128)(2,1)S(1)}, bf16[128,8,128]{2,0,1:T(8,128)(2,1)S(1)}, u32[]{:S(2)}, u32[]{:S(2)}) collective-permute-start(bf16[128,8,128]{2,0,1:T(8,128)(2,1)S(1)} %copy.135), channel_id=1, source_target_pairs={{0,4},{1,5},{2,6},{3,7},{4,8},{5,9},{6,10},{7,11},{8,12},{9,13},{1... | collective-permute-start | bytes 786440 | tf_op jit(solution)/shard_map/ppermute | solution.py:16
  156.4 12.3 %collective-permute-start.5 = (bf16[128,8,128]{2,0,1:T(8,128)(2,1)S(1)}, bf16[128,8,128]{2,0,1:T(8,128)(2,1)S(1)}, u32[]{:S(2)}, u32[]{:S(2)}) collective-permute-start(bf16[128,8,128]{2,0,1:T(8,128)(2,1)S(1)} %copy.135), channel_id=1, source_target_pairs={{0,3},{1,4},{2,5},{3,6},{4,7},{5,8},{6,9},{7,10},{8,11},{9,12},{10... | collective-permute-start | bytes 786440 | tf_op jit(solution)/shard_map/ppermute | solution.py:16
  207.0 21.0 %collective-permute-start.31 = (f32[128,8,128]{2,0,1:T(8,128)}, f32[128,8,128]{2,0,1:T(8,128)S(1)}, u32[]{:S(2)}, u32[]{:S(2)}) collective-permute-start(f32[128,8,128]{2,0,1:T(8,128)} %get-tuple-element.27), channel_id=1, source_target_pairs={{8,0},{9,1},{10,2},{11,3},{12,4},{13,5},{14,6},{15,7},{24,16},{25,... | collective-permute-start | bytes 1572872 | tf_op jit(solution)/shard_map/ppermute | solution.py:16
  208.3 36.1 %collective-permute-start.30 = (f32[128,8,128]{2,0,1:T(8,128)S(1)}, f32[128,8,128]{2,0,1:T(8,128)S(1)}, u32[]{:S(2)}, u32[]{:S(2)}) collective-permute-start(f32[128,8,128]{2,0,1:T(8,128)S(1)} %get-tuple-element.28), channel_id=1, source_target_pairs={{7,0},{8,1},{9,2},{10,3},{11,4},{12,5},{13,6},{14,7},{15,8},{23,16... | collective-permute-start | bytes 1572872 | tf_op jit(solution)/shard_map/ppermute | solution.py:16
  209.6 59.1 %collective-permute-start.29 = (f32[128,8,128]{2,0,1:T(8,128)S(1)}, f32[128,8,128]{2,0,1:T(8,128)S(1)}, u32[]{:S(2)}, u32[]{:S(2)}) collective-permute-start(f32[128,8,128]{2,0,1:T(8,128)S(1)} %get-tuple-element.29), channel_id=1, source_target_pairs={{6,0},{7,1},{8,2},{9,3},{10,4},{11,5},{12,6},{13,7},{14,8},{15,9},... | collective-permute-start | bytes 1572872 | tf_op jit(solution)/shard_map/ppermute | solution.py:16
  211.5 68.1 %collective-permute-start.28 = (f32[128,8,128]{2,0,1:T(8,128)}, f32[128,8,128]{2,0,1:T(8,128)S(1)}, u32[]{:S(2)}, u32[]{:S(2)}) collective-permute-start(f32[128,8,128]{2,0,1:T(8,128)} %get-tuple-element.30), channel_id=1, source_target_pairs={{5,0},{6,1},{7,2},{8,3},{9,4},{10,5},{11,6},{12,7},{13,8},{14,9},{... | collective-permute-start | bytes 1572872 | tf_op jit(solution)/shard_map/ppermute | solution.py:16
  213.9 83.5 %collective-permute-start.27 = (f32[128,8,128]{2,0,1:T(8,128)S(1)}, f32[128,8,128]{2,0,1:T(8,128)S(1)}, u32[]{:S(2)}, u32[]{:S(2)}) collective-permute-start(f32[128,8,128]{2,0,1:T(8,128)S(1)} %get-tuple-element.31), channel_id=1, source_target_pairs={{4,0},{5,1},{6,2},{7,3},{8,4},{9,5},{10,6},{11,7},{12,8},{13,9},{1... | collective-permute-start | bytes 1572872 | tf_op jit(solution)/shard_map/ppermute | solution.py:16
  227.9 119.5 %collective-permute-start.26 = (f32[128,8,128]{2,0,1:T(8,128)S(1)}, f32[128,8,128]{2,0,1:T(8,128)S(1)}, u32[]{:S(2)}, u32[]{:S(2)}) collective-permute-start(f32[128,8,128]{2,0,1:T(8,128)S(1)} %get-tuple-element.32), channel_id=1, source_target_pairs={{3,0},{4,1},{5,2},{6,3},{7,4},{8,5},{9,6},{10,7},{11,8},{12,9},{13... | collective-permute-start | bytes 1572872 | tf_op jit(solution)/shard_map/ppermute | solution.py:16
  244.3 133.3 %collective-permute-start.25 = (f32[128,8,128]{2,0,1:T(8,128)S(1)}, f32[128,8,128]{2,0,1:T(8,128)S(1)}, u32[]{:S(2)}, u32[]{:S(2)}) collective-permute-start(f32[128,8,128]{2,0,1:T(8,128)S(1)} %get-tuple-element.33), channel_id=1, source_target_pairs={{2,0},{3,1},{4,2},{5,3},{6,4},{7,5},{8,6},{9,7},{10,8},{11,9},{12,... | collective-permute-start | bytes 1572872 | tf_op jit(solution)/shard_map/ppermute | solution.py:16
  268.7 110.8 %collective-permute-start.32 = (f32[128,8,128]{0,2,1:T(8,128)S(1)}, f32[128,8,128]{0,2,1:T(8,128)S(1)}, u32[]{:S(2)}, u32[]{:S(2)}) collective-permute-start(f32[128,8,128]{0,2,1:T(8,128)S(1)} %get-tuple-element.18), channel_id=1, source_target_pairs={{1,0},{2,1},{3,2},{4,3},{5,4},{6,5},{7,6},{8,7},{9,8},{10,9},{11,1... | collective-permute-start | bytes 1572872 | tf_op jit(solution)/shard_map/ppermute | solution.py:16
  279.6 101.9 %collective-permute-start.39 = (f32[128,8,128]{0,2,1:T(8,128)S(1)}, f32[128,8,128]{0,2,1:T(8,128)S(1)}, u32[]{:S(2)}, u32[]{:S(2)}) collective-permute-start(f32[128,8,128]{0,2,1:T(8,128)S(1)} %get-tuple-element.19), channel_id=1, source_target_pairs={{8,0},{9,1},{10,2},{11,3},{12,4},{13,5},{14,6},{15,7},{24,16},{25,... | collective-permute-start | bytes 1572872 | tf_op jit(solution)/shard_map/ppermute | solution.py:16
  297.4 86.0 %collective-permute-start.38 = (f32[128,8,128]{0,2,1:T(8,128)S(1)}, f32[128,8,128]{0,2,1:T(8,128)S(1)}, u32[]{:S(2)}, u32[]{:S(2)}) collective-permute-start(f32[128,8,128]{0,2,1:T(8,128)S(1)} %get-tuple-element.20), channel_id=1, source_target_pairs={{7,0},{8,1},{9,2},{10,3},{11,4},{12,5},{13,6},{14,7},{15,8},{23,16... | collective-permute-start | bytes 1572872 | tf_op jit(solution)/shard_map/ppermute | solution.py:16
  347.4 48.0 %collective-permute-start.37 = (f32[128,8,128]{0,2,1:T(8,128)}, f32[128,8,128]{0,2,1:T(8,128)}, u32[]{:S(2)}, u32[]{:S(2)}) collective-permute-start(f32[128,8,128]{0,2,1:T(8,128)} %get-tuple-element.21), channel_id=1, source_target_pairs={{6,0},{7,1},{8,2},{9,3},{10,4},{11,5},{12,6},{13,7},{14,8},{15,9},... | collective-permute-start | bytes 1572872 | tf_op jit(solution)/shard_map/ppermute | solution.py:16
  377.6 17.9 %collective-permute-start.36 = (f32[128,8,128]{0,2,1:T(8,128)}, f32[128,8,128]{0,2,1:T(8,128)}, u32[]{:S(2)}, u32[]{:S(2)}) collective-permute-start(f32[128,8,128]{0,2,1:T(8,128)} %get-tuple-element.22), channel_id=1, source_target_pairs={{5,0},{6,1},{7,2},{8,3},{9,4},{10,5},{11,6},{12,7},{13,8},{14,9},{... | collective-permute-start | bytes 1572872 | tf_op jit(solution)/shard_map/ppermute | solution.py:16
  379.5 15.9 %collective-permute-start.35 = (f32[128,8,128]{0,2,1:T(8,128)}, f32[128,8,128]{0,2,1:T(8,128)}, u32[]{:S(2)}, u32[]{:S(2)}) collective-permute-start(f32[128,8,128]{0,2,1:T(8,128)} %get-tuple-element.23), channel_id=1, source_target_pairs={{4,0},{5,1},{6,2},{7,3},{8,4},{9,5},{10,6},{11,7},{12,8},{13,9},{1... | collective-permute-start | bytes 1572872 | tf_op jit(solution)/shard_map/ppermute | solution.py:16
  381.5 56.0 %collective-permute-start.34 = (f32[128,8,128]{0,2,1:T(8,128)}, f32[128,8,128]{0,2,1:T(8,128)}, u32[]{:S(2)}, u32[]{:S(2)}) collective-permute-start(f32[128,8,128]{0,2,1:T(8,128)} %get-tuple-element.24), channel_id=1, source_target_pairs={{3,0},{4,1},{5,2},{6,3},{7,4},{8,5},{9,6},{10,7},{11,8},{12,9},{13... | collective-permute-start | bytes 1572872 | tf_op jit(solution)/shard_map/ppermute | solution.py:16
  383.4 74.7 %collective-permute-start.33 = (f32[128,8,128]{0,2,1:T(8,128)S(1)}, f32[128,8,128]{0,2,1:T(8,128)}, u32[]{:S(2)}, u32[]{:S(2)}) collective-permute-start(f32[128,8,128]{0,2,1:T(8,128)S(1)} %get-tuple-element.25), channel_id=1, source_target_pairs={{2,0},{3,1},{4,2},{5,3},{6,4},{7,5},{8,6},{9,7},{10,8},{11,9},{12,... | collective-permute-start | bytes 1572872 | tf_op jit(solution)/shard_map/ppermute | solution.py:16
  (46 other events, 1210.4 us)
where the time goes:
time: 463 us; the launch traced here: 461 us
  waiting for transfers between devices  251 us (54%)
  starting transfers between devices  149 us (32%)
  matrix products  22 us (5%)
  local copies, waits for them, and re-layouts  20.4 us (4%)
  other arithmetic  16.7 us (4%)
    ppermute x40, waiting for transfers between devices, from_behind(): return lax.ppermute(block, axis, route)  251 us
    ppermute x40, starting transfers between devices, from_behind(): return lax.ppermute(block, axis, route)  149 us
  transfers between devices with their start and end apart: 40, of which 17 were waited for; matrix products, arithmetic and copies ran while one was open for 4% of the time, Pallas kernels for 0%

commit v1 on v0

v1 whole, which is shorter than its diff:
```python
import functools

import jax
import jax.numpy as jnp
from jax import lax
from jax.experimental import pallas as pl
from jax.experimental.pallas import tpu as pltpu
from jax.sharding import PartitionSpec as P

WINDOW = 1024
SCALE = 168.0 ** (-0.5)
NEGATIVE = -1e30
MESH = pl.DeviceIdType.MESH
R = 4
T = 128
D = 128
BF = jnp.bfloat16
F32 = jnp.float32
KV_A, QG_A, ME_A, KV_1, ME_1, KV_2, ME_2, RW, B2, B1, OQ, OKV = range(12)


def dot(a, b, ca, cb):
    return lax.dot_general(a, b, (((ca,), (cb,)), ((), ())), preferred_element_type=F32)


def kernel(
    n, kv_in, qg_in, me_in, ro_ref, oq, okv,
    kvb, qgb, meta, segc, rob, bias, pb, ob, rwb, acc, gqb, b2s, b2r, b1s, b1r, kvs,
    ssem, rsem,
):
    planes = n // R
    me = lax.axis_index("context")
    r = lax.rem(me, R)
    p = lax.div(me, R)
    base = p * R
    has_dn = p >= 1
    has_up = p < planes - 1
    has2 = p >= 2
    mid = jnp.logical_and(has_dn, has_up)
    up = me + R
    dn = me - R

    def send(k, src, dst, to, s, d):
        pltpu.make_async_remote_copy(
            src_ref=src, dst_ref=dst, send_sem=ssem.at[k, s], recv_sem=rsem.at[k, d],
            device_id={"context": to}, device_id_type=MESH,
        ).start()

    def wait_recv(k, c, ref):
        pltpu.make_async_copy(ref, ref, rsem.at[k, c]).wait()

    def wait_send(k, c, ref):
        pltpu.make_async_copy(ref, ref, ssem.at[k, c]).wait()

    def peer(o):
        return lax.rem(r + o, R)

    def rows(start):
        return pl.ds(pl.multiple_of(start, T), T)

    def kchunk(c):
        return kvb.at[rows(c * T)]

    def qchunk(c):
        return qgb.at[rows(c * T)]

    barrier = pltpu.get_barrier_semaphore()
    for o in range(1, R):
        pl.semaphore_signal(barrier, inc=1, device_id={"context": base + peer(o)}, device_id_type=MESH)

    @pl.when(has_dn)
    def _():
        pl.semaphore_signal(barrier, inc=1, device_id={"context": dn}, device_id_type=MESH)

    @pl.when(has_up)
    def _():
        pl.semaphore_signal(barrier, inc=1, device_id={"context": up}, device_id_type=MESH)

    pltpu.make_async_copy(kv_in.at[r], kchunk(8 + r), rsem.at[KV_A, r]).start()
    pltpu.make_async_copy(me_in, meta.at[8 + r], rsem.at[ME_A, r]).start()
    pltpu.make_async_copy(qg_in.at[r], qchunk(r), rsem.at[QG_A, r]).start()
    pl.semaphore_wait(barrier, R - 1 + has_dn.astype(jnp.int32) + has_up.astype(jnp.int32))

    for o in range(1, R):
        d = peer(o)
        send(KV_A, kv_in.at[d], kchunk(8 + r), base + d, d, r)
        send(ME_A, me_in, meta.at[8 + r], base + d, d, r)
    for o in range(1, R):
        d = peer(o)
        send(QG_A, qg_in.at[d], qchunk(r), base + d, d, r)

    for c in range(R - 1, -1, -1):
        wait_recv(KV_A, c, kchunk(8 + c))
        wait_recv(ME_A, c, meta.at[8 + c])

        @pl.when(has_up)
        def _():
            send(KV_1, kchunk(8 + c), kchunk(4 + c), up, c, c)
            send(ME_1, meta.at[8 + c], meta.at[4 + c], up, c, c)

    @pl.when(jnp.logical_not(has_dn))
    def _():
        kvb[4 * T : 8 * T] = jnp.zeros((4 * T, 4 * D), BF)
        meta[4:8] = jnp.full((4, 8, T), -1.0, F32)

    @pl.when(jnp.logical_not(has2))
    def _():
        kvb[0 : 4 * T] = jnp.zeros((4 * T, 4 * D), BF)
        meta[0:4] = jnp.full((4, 8, T), -1.0, F32)

    acc[...] = jnp.zeros_like(acc)
    for h in range(4):
        rob[h] = jnp.broadcast_to(ro_ref[pl.ds(4 * r + h, 1), :], (D, D)).T

    for c in range(R - 1, -1, -1):
        @pl.when(has_dn)
        def _():
            wait_recv(KV_1, c, kchunk(4 + c))
            wait_recv(ME_1, c, meta.at[4 + c])

        @pl.when(mid)
        def _():
            send(KV_2, kchunk(4 + c), kchunk(c), up, c, c)
            send(ME_2, meta.at[4 + c], meta.at[c], up, c, c)

    for c in range(R):
        wait_recv(QG_A, c, qchunk(c))

    def seg_column(c):
        segc[rows(c * T)] = jnp.broadcast_to(meta[c, 0:1, :], (T, T)).T

    def seg_body(c, carry):
        seg_column(c + 4)
        return carry

    lax.fori_loop(0, 8, seg_body, 0)

    def win(i):
        return pl.ds(pl.multiple_of(i * T, T), WINDOW + T)

    def two(ref, i, g, at):
        lane = at + 2 * g * D
        return jnp.concatenate(
            [ref[rows(i * T), lane : lane + D], ref[rows(i * T), lane + D : lane + 2 * D]], axis=0
        )

    def forward(step, carry):
        i = R - 1 - step

        @pl.when(has2)
        def _():
            wait_recv(KV_2, i, kchunk(i))
            wait_recv(ME_2, i, meta.at[i])

        seg_column(i)
        seg_q = meta[8 + i, 0:1, :]
        for j in range(9):
            ok = segc[rows((i + j) * T)] == seg_q
            if j in (0, 8):
                kk = lax.broadcasted_iota(jnp.int32, (T, T), 0)
                tq = lax.broadcasted_iota(jnp.int32, (T, T), 1)
                ok = jnp.logical_and(ok, kk > tq if j == 0 else kk <= tq)
            bias[j * T : (j + 1) * T] = jnp.where(ok, 0.0, NEGATIVE)
        total = jnp.zeros((1, T), F32)
        for g in range(2):
            q2 = two(qgb, i, g, 0)
            s = dot(kvb[win(i), g * D : (g + 1) * D], q2, 1, 1) * SCALE
            b = bias[...]
            s = s + jnp.concatenate([b, b], axis=1)
            e = jnp.exp(s - jnp.max(s, axis=0, keepdims=True))
            low = (e * (1.0 / jnp.sum(e, axis=0, keepdims=True))).astype(BF)
            pb[2 * i + g] = low
            o = dot(kvb[win(i), (2 + g) * D : (3 + g) * D], low, 0, 0)
            ob[2 * i + g] = o
            w = o[:, :T] * rob[2 * g] + o[:, T:] * rob[2 * g + 1]
            total = total + jnp.sum(w, axis=0, keepdims=True)
        rwb[r, i] = jnp.broadcast_to(total, (8, T))
        return carry

    lax.fori_loop(0, R, forward, 0)

    for o in range(1, R):
        send(RW, rwb.at[r], rwb.at[r], base + peer(o), peer(o), r)
    for o in range(1, R):
        wait_recv(RW, peer(o), rwb.at[peer(o)])

    def packed(start):
        return jnp.concatenate(
            [acc[rows(start), : 2 * D] * SCALE, acc[rows(start), 2 * D :]], axis=1
        )

    def backward(i, carry):
        reward = jnp.sum(rwb[:, i, 0:1, :], axis=0)
        live = meta[8 + i, 1:2, :]
        pg = live * (jax.nn.sigmoid(reward) - meta[8 + i, 2:3, :])
        for g in range(2):
            q2 = two(qgb, i, g, 0)
            go = two(qgb, i, g, 4 * D).astype(F32).T
            ga_t = jnp.concatenate(
                [
                    live * go[:, :T] + pg * rob[2 * g],
                    live * go[:, T:] + pg * rob[2 * g + 1],
                ],
                axis=1,
            ).astype(BF)
            ga_f = ga_t.astype(F32)
            ga2 = ga_f.T.astype(BF)
            delta = jnp.sum(ga_f * ob[2 * i + g], axis=0, keepdims=True)
            low = pb[2 * i + g]
            dp = dot(kvb[win(i), (2 + g) * D : (3 + g) * D], ga_t, 1, 0)
            ds = (low.astype(F32) * (dp - delta)).astype(BF)
            gq = dot(kvb[win(i), g * D : (g + 1) * D], ds, 0, 0) * SCALE
            gq = gq.T.astype(BF)
            gqb[i, :, 2 * g * D : (2 * g + 1) * D] = gq[:T]
            gqb[i, :, (2 * g + 1) * D : (2 * g + 2) * D] = gq[T:]
            acc[win(i), g * D : (g + 1) * D] += dot(ds, q2, 1, 0)
            acc[win(i), (2 + g) * D : (3 + g) * D] += dot(low, ga2, 1, 0)

        @pl.when(i == r)
        def _():
            pltpu.make_async_copy(gqb.at[i], oq.at[i], rsem.at[OQ, i]).start()

        @pl.when(i != r)
        def _():
            send(OQ, gqb.at[i], oq.at[r], base + i, i, r)

        @pl.when(has2)
        def _():
            b2s[i] = packed(i * T).astype(BF)
            send(B2, b2s.at[i], b2r.at[i], dn, i, i)

        return carry

    lax.fori_loop(0, R, backward, 0)

    def near(c, carry):
        @pl.when(mid)
        def _():
            wait_recv(B2, c, b2r.at[c])
            b1s[c] = (packed((4 + c) * T) + b2r[c].astype(F32)).astype(BF)

        @pl.when(jnp.logical_and(has_dn, jnp.logical_not(has_up)))
        def _():
            b1s[c] = packed((4 + c) * T).astype(BF)

        @pl.when(has_dn)
        def _():
            send(B1, b1s.at[c], b1r.at[c], dn, c, c)

        return carry

    lax.fori_loop(0, R, near, 0)

    def own(c, carry):
        @pl.when(has_up)
        def _():
            wait_recv(B1, c, b1r.at[c])
            kvs[c] = (packed((8 + c) * T) + b1r[c].astype(F32)).astype(BF)

        @pl.when(jnp.logical_not(has_up))
        def _():
            kvs[c] = packed((8 + c) * T).astype(BF)

        @pl.when(c == r)
        def _():
            pltpu.make_async_copy(kvs.at[c], okv.at[c], rsem.at[OKV, c]).start()

        @pl.when(c != r)
        def _():
            send(OKV, kvs.at[c], okv.at[r], base + c, c, r)

        return carry

    lax.fori_loop(0, R, own, 0)

    for o in range(1, R):
        d = peer(o)
        wait_send(KV_A, d, kchunk(8))
        wait_send(ME_A, d, meta.at[8])
        wait_send(QG_A, d, qchunk(0))
        wait_send(RW, d, rwb.at[0])
        wait_send(OQ, d, gqb.at[0])
        wait_send(OKV, d, kvs.at[0])
    for c in range(R):
        @pl.when(has_up)
        def _():
            wait_send(KV_1, c, kchunk(8 + c))
            wait_send(ME_1, c, meta.at[8 + c])

        @pl.when(mid)
        def _():
            wait_send(KV_2, c, kchunk(4 + c))
            wait_send(ME_2, c, meta.at[4 + c])

        @pl.when(has2)
        def _():
            wait_send(B2, c, b2s.at[c])

        @pl.when(has_dn)
        def _():
            wait_send(B1, c, b1s.at[c])

        wait_recv(OQ, c, oq.at[c])
        wait_recv(OKV, c, okv.at[c])


def local(n, queries, keys, values, grad_out, readout, segments, loss_mask, labels):
    tokens, heads, dim = queries.shape
    kv = keys.shape[1]

    def parts(*arrays):
        flat = [a.reshape(tokens, R, -1) for a in arrays]
        return jnp.concatenate(flat, axis=2).transpose(1, 0, 2)

    kv_in = parts(keys, values)
    qg_in = parts(queries, grad_out)
    meta = jnp.stack([segments, loss_mask, labels] + [segments] * 5).astype(F32)
    any_spec = pl.BlockSpec(memory_space=pl.ANY)
    vmem = pltpu.VMEM
    span = WINDOW + R * T
    oq, okv = pl.pallas_call(
        functools.partial(kernel, n),
        out_shape=[
            jax.ShapeDtypeStruct((R, T, 4 * D), BF),
            jax.ShapeDtypeStruct((R, T, 4 * D), BF),
        ],
        in_specs=[any_spec, any_spec, any_spec, pl.BlockSpec(memory_space=pltpu.VMEM)],
        out_specs=[any_spec, any_spec],
        scratch_shapes=[
            vmem((span, 4 * D), BF),
            vmem((R * T, 8 * D), BF),
            vmem((12, 8, T), F32),
            vmem((span, T), F32),
            vmem((4, D, D), F32),
            vmem((WINDOW + T, T), F32),
            vmem((8, WINDOW + T, 2 * T), BF),
            vmem((8, D, 2 * T), F32),
            vmem((R, R, 8, T), F32),
            vmem((span, 4 * D), F32),
            vmem((R, T, 4 * D), BF),
            vmem((R, T, 4 * D), BF),
            vmem((R, T, 4 * D), BF),
            vmem((R, T, 4 * D), BF),
            vmem((R, T, 4 * D), BF),
            vmem((R, T, 4 * D), BF),
            pltpu.SemaphoreType.DMA((12, R)),
            pltpu.SemaphoreType.DMA((12, R)),
        ],
        compiler_params=pltpu.CompilerParams(
            collective_id=0, has_side_effects=True, vmem_limit_bytes=48 * 1024 * 1024
        ),
    )(kv_in, qg_in, meta, readout)
    grad_queries = oq.transpose(1, 0, 2).reshape(tokens, heads, dim)
    both = okv.transpose(1, 0, 2)
    grad_keys = both[:, :, : 2 * D].reshape(tokens, kv, dim)
    grad_values = both[:, :, 2 * D :].reshape(tokens, kv, dim)
    return grad_queries, grad_keys, grad_values


def solution(mesh):
    tok = P(("groups", "context"), None, None)
    row = P(("groups", "context"))
    return jax.shard_map(
        functools.partial(local, mesh.shape["context"]),
        mesh=mesh,
        in_specs=(tok, tok, tok, tok, P(), row, row, row),
        out_specs=(tok, tok, tok),
        check_vma=False,
    )
```

time: 463 us -> 76.4 us (0.17)
  the two profiles are of different devices: /device:TPU:12 before, /device:TPU:15 now
where the time goes in v1:
time: 76.4 us; the launch traced here: 76.1 us
  Pallas kernels  66.2 us (87%)
  local copies, waits for them, and re-layouts  9.06 us (12%)
    pallas_call x1, Pallas kernels, local(): pl.pallas_call(functools.partial(kernel, n), out_shape=[jax.ShapeDtypeStr...  66.2 us
    unnamed x15, local copies, waits for them, and re-layouts  6.8 us

profile of v1, /device:TPU:15, one launch (start us, length us, event | category | flops | bytes accessed | tf_op | source)
XLA Modules:
  0.0 76.1 jit_solution(14087266210618343509)
XLA Ops:
  0.6 0.0 copy-start.3
  0.6 0.9 %stack.20 = s32[8,128]{1,0:T(8,128)S(1)} concatenate(s32[1,128]{1,0:T(1,128)} %bitcast.25, s32[1,128]{1,0:T(1,128)} %bitcast.31, s32[1,128]{1,0:T(1,128)} %bitcast.32, s32[1,128]{1,0:T(1,128)} %bitcast.26, s32[1,128]{1,0:T(1,128)} %bitcast.27, s32[1,128]{1,0:T(1,128)} %bitcast.28, s32[1,128]{1,0:T(1,128)} %bitcast.29, s32[1,128]{1,0:T(1,128)} %bitcast.30), dimensions={0} | concatenate | bytes 8192 | tf_op jit(solution)/shard_map/stack | solution.py:317
  1.5 1.2 %copy.11 = bf16[128,8,128]{0,2,1:T(8,128)(2,1)S(1)} copy(bf16[128,8,128]{2,1,0:T(8,128)(2,1)} %param.9) | data formatting | bytes 524288 | tf_op args[1]
  2.7 0.1 copy.13
  2.9 0.0 copy-done.3
  2.9 0.0 copy-start.1
  2.9 0.2 copy.12
  3.1 0.1 copy.14
  3.3 0.6 copy-done.1
  3.9 0.0 copy-start.2
  3.9 0.5 copy.15
  4.4 0.2 copy.17
  4.6 0.4 copy-done.2
  4.9 0.5 copy.16
  5.4 0.2 copy.18
  5.6 0.0 copy-start
  5.7 0.1 maximum_bitcast_fusion.qg_in
  5.8 0.6 copy-done
  6.3 66.2 %shard_map.103 = (bf16[4,128,512]{2,1,0:T(8,128)(2,1)S(1)}, bf16[4,128,512]{2,1,0:T(8,128)(2,1)S(1)}) custom-call(bf16[4,128,512]{2,1,0:T(8,128)(2,1)S(1)} %maximum_bitcast_fusion.1.kv_in, bf16[4,128,1024]{2,1,0:T(8,128)(2,1)S(1)} %maximum_bitcast_fusion.qg_in, f32[8,128]{1,0:T(8,128)S(1)} %convert_element_type.3.me_in, f32[16,128]{1,0:T(8,128)S(1)} %copy-done), custom_call_target="tpu_custom_call" | custom-call | tf_op jit(solution)/shard_map/pallas_call | solution.py:321
  72.5 0.3 copy.19
  72.8 1.2 %copy.22 = bf16[128,16,128]{2,1,0:T(8,128)(2,1)} copy(bf16[128,16,128]{0,2,1:T(8,128)(2,1)S(1)} %bitcast.18) | data formatting | bytes 1048576
  74.0 0.2 copy.21
  74.2 0.9 %copy.24 = bf16[128,8,128]{2,1,0:T(8,128)(2,1)} copy(bf16[128,8,128]{0,2,1:T(8,128)(2,1)S(1)} %bitcast.21) | data formatting | bytes 524288
  75.1 0.2 copy.20
  75.2 0.9 %copy.23 = bf16[128,8,128]{2,1,0:T(8,128)(2,1)} copy(bf16[128,8,128]{0,2,1:T(8,128)(2,1)S(1)} %bitcast.22) | data formatting | bytes 524288
  (3 shorter events, 0.1 us)
Async XLA Ops:
  0.6 2.2 %copy-start.3 = (bf16[128,8,128]{2,1,0:T(8,128)(2,1)S(1)}, bf16[128,8,128]{2,1,0:T(8,128)(2,1)}, u32[]{:S(2)}) copy-start(bf16[128,8,128]{2,1,0:T(8,128)(2,1)} %param.10) | copy-start | bytes 786436
  2.9 1.0 %copy-start.1 = (bf16[128,16,128]{2,1,0:T(8,128)(2,1)S(1)}, bf16[128,16,128]{2,1,0:T(8,128)(2,1)}, u32[]{:S(2)}) copy-start(bf16[128,16,128]{2,1,0:T(8,128)(2,1)} %param.8) | copy-start | bytes 1572868
  3.9 1.0 %copy-start.2 = (bf16[128,16,128]{2,1,0:T(8,128)(2,1)S(1)}, bf16[128,16,128]{2,1,0:T(8,128)(2,1)}, u32[]{:S(2)}) copy-start(bf16[128,16,128]{2,1,0:T(8,128)(2,1)} %param.11) | copy-start | bytes 1572868
  5.6 0.7 copy-start

commit v2 on v1

--- a/solution.py
+++ b/solution.py
@@ -85,18 +85,19 @@
         d = peer(o)
         send(KV_A, kv_in.at[d], kchunk(8 + r), base + d, d, r)
         send(ME_A, me_in, meta.at[8 + r], base + d, d, r)
+    for k in range(R):
+        c = lax.rem(lax.div(r, 2) + k // 2, 2) * 2 + lax.rem(r + k, 2)
+        wait_recv(KV_A, c, kchunk(8 + c))
+        wait_recv(ME_A, c, meta.at[8 + c])
+
+        @pl.when(has_up)
+        def _():
+            send(KV_1, kchunk(8 + c), kchunk(4 + c), up, c, c)
+            send(ME_1, meta.at[8 + c], meta.at[4 + c], up, c, c)
+
     for o in range(1, R):
         d = peer(o)
         send(QG_A, qg_in.at[d], qchunk(r), base + d, d, r)
-
-    for c in range(R - 1, -1, -1):
-        wait_recv(KV_A, c, kchunk(8 + c))
-        wait_recv(ME_A, c, meta.at[8 + c])
-
-        @pl.when(has_up)
-        def _():
-            send(KV_1, kchunk(8 + c), kchunk(4 + c), up, c, c)
-            send(ME_1, meta.at[8 + c], meta.at[4 + c], up, c, c)
 
     @pl.when(jnp.logical_not(has_dn))
     def _():

time: 76.4 us -> 74.5 us (0.975)
  Pallas kernels: 66.2 us -> 64.2 us
    pallas_call x1, Pallas kernels: 66.2 us -> 64.2 us  [local(): pl.pallas_call(functools.partial(kernel, n), out_shape=[jax.ShapeDtypeStr...]
where the time goes in v2:
time: 74.5 us; the launch traced here: 74.2 us
  Pallas kernels  64.2 us (86%)
  local copies, waits for them, and re-layouts  9.06 us (12%)
  between operations  0.75 us (1%)
    pallas_call x1, Pallas kernels, local(): pl.pallas_call(functools.partial(kernel, n), out_shape=[jax.ShapeDtypeStr...  64.2 us
    unnamed x15, local copies, waits for them, and re-layouts  6.8 us

profile of v2, /device:TPU:15, one launch (start us, length us, event | category | flops | bytes accessed | tf_op | source)
XLA Modules:
  0.0 74.2 jit_solution(10244407303042754426)
XLA Ops:
  0.6 0.0 copy-start.3
  0.6 0.9 %stack.20 = s32[8,128]{1,0:T(8,128)S(1)} concatenate(s32[1,128]{1,0:T(1,128)} %bitcast.25, s32[1,128]{1,0:T(1,128)} %bitcast.31, s32[1,128]{1,0:T(1,128)} %bitcast.32, s32[1,128]{1,0:T(1,128)} %bitcast.26, s32[1,128]{1,0:T(1,128)} %bitcast.27, s32[1,128]{1,0:T(1,128)} %bitcast.28, s32[1,128]{1,0:T(1,128)} %bitcast.29, s32[1,128]{1,0:T(1,128)} %bitcast.30), dimensions={0} | concatenate | bytes 8192 | tf_op jit(solution)/shard_map/stack | solution.py:318
  1.5 1.2 %copy.11 = bf16[128,8,128]{0,2,1:T(8,128)(2,1)S(1)} copy(bf16[128,8,128]{2,1,0:T(8,128)(2,1)} %param.9) | data formatting | bytes 524288 | tf_op args[1]
  2.7 0.1 copy.13
  2.9 0.0 copy-done.3
  2.9 0.0 copy-start.1
  2.9 0.2 copy.12
  3.1 0.1 copy.14
  3.3 0.6 copy-done.1
  3.9 0.0 copy-start.2
  3.9 0.5 copy.15
  4.4 0.2 copy.17
  4.6 0.4 copy-done.2
  4.9 0.5 copy.16
  5.4 0.2 copy.18
  5.6 0.0 copy-start
  5.7 0.1 maximum_bitcast_fusion.qg_in
  5.8 0.6 copy-done
  6.3 64.2 %shard_map.103 = (bf16[4,128,512]{2,1,0:T(8,128)(2,1)S(1)}, bf16[4,128,512]{2,1,0:T(8,128)(2,1)S(1)}) custom-call(bf16[4,128,512]{2,1,0:T(8,128)(2,1)S(1)} %maximum_bitcast_fusion.1.kv_in, bf16[4,128,1024]{2,1,0:T(8,128)(2,1)S(1)} %maximum_bitcast_fusion.qg_in, f32[8,128]{1,0:T(8,128)S(1)} %convert_element_type.3.me_in, f32[16,128]{1,0:T(8,128)S(1)} %copy-done), custom_call_target="tpu_custom_call" | custom-call | tf_op jit(solution)/shard_map/pallas_call | solution.py:322
  70.6 0.3 copy.19
  70.9 1.2 %copy.22 = bf16[128,16,128]{2,1,0:T(8,128)(2,1)} copy(bf16[128,16,128]{0,2,1:T(8,128)(2,1)S(1)} %bitcast.18) | data formatting | bytes 1048576
  72.1 0.2 copy.21
  72.3 0.9 %copy.24 = bf16[128,8,128]{2,1,0:T(8,128)(2,1)} copy(bf16[128,8,128]{0,2,1:T(8,128)(2,1)S(1)} %bitcast.21) | data formatting | bytes 524288
  73.2 0.2 copy.20
  73.3 0.9 %copy.23 = bf16[128,8,128]{2,1,0:T(8,128)(2,1)} copy(bf16[128,8,128]{0,2,1:T(8,128)(2,1)S(1)} %bitcast.22) | data formatting | bytes 524288
  (3 shorter events, 0.1 us)
Async XLA Ops:
  0.6 2.2 %copy-start.3 = (bf16[128,8,128]{2,1,0:T(8,128)(2,1)S(1)}, bf16[128,8,128]{2,1,0:T(8,128)(2,1)}, u32[]{:S(2)}) copy-start(bf16[128,8,128]{2,1,0:T(8,128)(2,1)} %param.10) | copy-start | bytes 786436
  2.9 1.0 %copy-start.1 = (bf16[128,16,128]{2,1,0:T(8,128)(2,1)S(1)}, bf16[128,16,128]{2,1,0:T(8,128)(2,1)}, u32[]{:S(2)}) copy-start(bf16[128,16,128]{2,1,0:T(8,128)(2,1)} %param.8) | copy-start | bytes 1572868
  3.9 1.0 %copy-start.2 = (bf16[128,16,128]{2,1,0:T(8,128)(2,1)S(1)}, bf16[128,16,128]{2,1,0:T(8,128)(2,1)}, u32[]{:S(2)}) copy-start(bf16[128,16,128]{2,1,0:T(8,128)(2,1)} %param.11) | copy-start | bytes 1572868
  5.6 0.7 copy-start

commit v3 on v2

--- a/solution.py
+++ b/solution.py
@@ -10,6 +10,7 @@
 WINDOW = 1024
 SCALE = 168.0 ** (-0.5)
 NEGATIVE = -1e30
+LOG2E = 1.4426950408889634
 MESH = pl.DeviceIdType.MESH
 R = 4
 T = 128
@@ -24,8 +25,9 @@
 
 
 def kernel(
-    n, kv_in, qg_in, me_in, ro_ref, oq, okv,
+    n, kv_in, qg_in, seg_ref, live_ref, lab_ref, ro_ref, oq, okv,
     kvb, qgb, meta, segc, rob, bias, pb, ob, rwb, acc, gqb, b2s, b2r, b1s, b1r, kvs,
+    me_in, kvt, sb, dsb, inv,
     ssem, rsem,
 ):
     planes = n // R
@@ -76,6 +78,9 @@
     def _():
         pl.semaphore_signal(barrier, inc=1, device_id={"context": up}, device_id_type=MESH)
 
+    me_in[...] = jnp.concatenate(
+        [seg_ref[...], live_ref[...], lab_ref[...], jnp.zeros((5, T), jnp.int32)], axis=0
+    ).astype(F32)
     pltpu.make_async_copy(kv_in.at[r], kchunk(8 + r), rsem.at[KV_A, r]).start()
     pltpu.make_async_copy(me_in, meta.at[8 + r], rsem.at[ME_A, r]).start()
     pltpu.make_async_copy(qg_in.at[r], qchunk(r), rsem.at[QG_A, r]).start()
@@ -129,6 +134,7 @@
 
     def seg_column(c):
         segc[rows(c * T)] = jnp.broadcast_to(meta[c, 0:1, :], (T, T)).T
+        kvt[:, rows(c * T)] = kvb[rows(c * T)].T
 
     def seg_body(c, carry):
         seg_column(c + 4)
@@ -165,13 +171,27 @@
         total = jnp.zeros((1, T), F32)
         for g in range(2):
             q2 = two(qgb, i, g, 0)
-            s = dot(kvb[win(i), g * D : (g + 1) * D], q2, 1, 1) * SCALE
-            b = bias[...]
-            s = s + jnp.concatenate([b, b], axis=1)
-            e = jnp.exp(s - jnp.max(s, axis=0, keepdims=True))
-            low = (e * (1.0 / jnp.sum(e, axis=0, keepdims=True))).astype(BF)
-            pb[2 * i + g] = low
-            o = dot(kvb[win(i), (2 + g) * D : (3 + g) * D], low, 0, 0)
+            top = None
+            for j in range(9):
+                at = slice(j * T, (j + 1) * T)
+                raw = dot(kvb[rows((i + j) * T), g * D : (g + 1) * D], q2, 1, 1)
+                b = bias[at]
+                x = raw * (SCALE * LOG2E) + jnp.concatenate([b, b], axis=1)
+                sb[g, at] = x
+                m = jnp.max(x.reshape(T // 8, 8, 2 * T), axis=0)
+                top = m if top is None else jnp.maximum(top, m)
+            top = jnp.max(top, axis=0, keepdims=True)
+            total_e = None
+            for j in range(9):
+                at = slice(j * T, (j + 1) * T)
+                e = jnp.exp2(sb[g, at] - top)
+                pb[2 * i + g, at] = e.astype(BF)
+                m = jnp.sum(e.reshape(T // 8, 8, 2 * T), axis=0)
+                total_e = m if total_e is None else total_e + m
+            part = 1.0 / jnp.sum(total_e, axis=0, keepdims=True)
+            inv[2 * i + g] = jnp.broadcast_to(part, (8, 2 * T))
+            vt = kvt[(2 + g) * D : (3 + g) * D, win(i)]
+            o = dot(vt, pb[2 * i + g], 1, 0) * part
             ob[2 * i + g] = o
             w = o[:, :T] * rob[2 * g] + o[:, T:] * rob[2 * g + 1]
             total = total + jnp.sum(w, axis=0, keepdims=True)
@@ -205,17 +225,22 @@
                 axis=1,
             ).astype(BF)
             ga_f = ga_t.astype(F32)
-            ga2 = ga_f.T.astype(BF)
-            delta = jnp.sum(ga_f * ob[2 * i + g], axis=0, keepdims=True)
-            low = pb[2 * i + g]
-            dp = dot(kvb[win(i), (2 + g) * D : (3 + g) * D], ga_t, 1, 0)
-            ds = (low.astype(F32) * (dp - delta)).astype(BF)
-            gq = dot(kvb[win(i), g * D : (g + 1) * D], ds, 0, 0) * SCALE
+            part = inv[2 * i + g, 0:1, :]
+            delta = jnp.sum(ga_f * ob[2 * i + g], axis=0, keepdims=True) * part
+            ga2 = (ga_f * part).T.astype(BF)
+            for j in range(9):
+                at = slice(j * T, (j + 1) * T)
+                here = rows((i + j) * T)
+                low = pb[2 * i + g, at]
+                dp = dot(kvb[here, (2 + g) * D : (3 + g) * D], ga_t, 1, 0)
+                ds = (low.astype(F32) * (dp * part - delta)).astype(BF)
+                dsb[g, at] = ds
+                acc[here, g * D : (g + 1) * D] += dot(ds, q2, 1, 0)
+                acc[here, (2 + g) * D : (3 + g) * D] += dot(low, ga2, 1, 0)
+            gq = dot(kvt[g * D : (g + 1) * D, win(i)], dsb[g], 1, 0) * SCALE
             gq = gq.T.astype(BF)
             gqb[i, :, 2 * g * D : (2 * g + 1) * D] = gq[:T]
             gqb[i, :, (2 * g + 1) * D : (2 * g + 2) * D] = gq[T:]
-            acc[win(i), g * D : (g + 1) * D] += dot(ds, q2, 1, 0)
-            acc[win(i), (2 + g) * D : (3 + g) * D] += dot(low, ga2, 1, 0)
 
         @pl.when(i == r)
         def _():
@@ -315,7 +340,7 @@
 
     kv_in = parts(keys, values)
     qg_in = parts(queries, grad_out)
-    meta = jnp.stack([segments, loss_mask, labels] + [segments] * 5).astype(F32)
+    rows3 = [x.reshape(1, tokens) for x in (segments, loss_mask, labels)]
     any_spec = pl.BlockSpec(memory_space=pl.ANY)
     vmem = pltpu.VMEM
     span = WINDOW + R * T
@@ -325,7 +350,7 @@
             jax.ShapeDtypeStruct((R, T, 4 * D), BF),
             jax.ShapeDtypeStruct((R, T, 4 * D), BF),
         ],
-        in_specs=[any_spec, any_spec, any_spec, pl.BlockSpec(memory_space=pltpu.VMEM)],
+        in_specs=[any_spec, any_spec] + [pl.BlockSpec(memory_space=pltpu.VMEM)] * 4,
         out_specs=[any_spec, any_spec],
         scratch_shapes=[
             vmem((span, 4 * D), BF),
@@ -344,13 +369,18 @@
             vmem((R, T, 4 * D), BF),
             vmem((R, T, 4 * D), BF),
             vmem((R, T, 4 * D), BF),
+            vmem((8, T), F32),
+            vmem((4 * D, span), BF),
+            vmem((2, WINDOW + T, 2 * T), F32),
+            vmem((2, WINDOW + T, 2 * T), BF),
+            vmem((8, 8, 2 * T), F32),
             pltpu.SemaphoreType.DMA((12, R)),
             pltpu.SemaphoreType.DMA((12, R)),
         ],
         compiler_params=pltpu.CompilerParams(
             collective_id=0, has_side_effects=True, vmem_limit_bytes=48 * 1024 * 1024
         ),
-    )(kv_in, qg_in, meta, readout)
+    )(kv_in, qg_in, *rows3, readout)
     grad_queries = oq.transpose(1, 0, 2).reshape(tokens, heads, dim)
     both = okv.transpose(1, 0, 2)
     grad_keys = both[:, :, : 2 * D].reshape(tokens, kv, dim)

time: 74.5 us -> 74.6 us (level)
  Pallas kernels: 64.2 us -> 65.3 us
  local copies, waits for them, and re-layouts: 9.06 us -> 8.18 us
    pallas_call x1, Pallas kernels: 64.2 us -> 65.3 us  [local(): pl.pallas_call(functools.partial(kernel, n), out_shape=[jax.ShapeDtypeStr...]
    another operation x1 -> x0, local copies, waits for them, and re-layouts: 0.9 us -> none  [local(): meta = jnp.stack([segments, loss_mask, labels] + [segments] * 5).astype(F32)]
    unnamed x15 -> x21, local copies, waits for them, and re-layouts: 6.8 us -> 6.81 us
where the time goes in v3:
time: 74.6 us; the launch traced here: 74.4 us
  Pallas kernels  65.3 us (88%)
  local copies, waits for them, and re-layouts  8.18 us (11%)
  between operations  0.77 us (1%)
    pallas_call x1, Pallas kernels, local(): pl.pallas_call(functools.partial(kernel, n), out_shape=[jax.ShapeDtypeStr...  65.3 us
    unnamed x21, local copies, waits for them, and re-layouts  6.81 us

profile of v3, /device:TPU:15, one launch (start us, length us, event | category | flops | bytes accessed | tf_op | source)
XLA Modules:
  0.0 74.4 jit_solution(1118810502981285381)
XLA Ops:
  0.6 0.0 copy-start.6
  0.6 1.2 %copy.11 = bf16[128,8,128]{0,2,1:T(8,128)(2,1)S(1)} copy(bf16[128,8,128]{2,1,0:T(8,128)(2,1)} %param.9) | data formatting | bytes 524288 | tf_op args[1]
  1.8 0.1 copy.13
  2.0 0.0 copy-done.6
  2.0 0.0 copy-start.4
  2.0 0.2 copy.12
  2.2 0.1 copy.14
  2.4 0.6 copy-done.4
  3.0 0.0 copy-start.5
  3.0 0.5 copy.15
  3.5 0.2 copy.17
  3.7 0.4 copy-done.5
  4.1 0.5 copy.16
  4.5 0.2 copy.18
  4.8 0.0 copy-start
  4.8 0.0 copy-start.1
  4.8 0.0 copy-start.2
  4.8 0.0 copy-start.3
  4.8 0.1 maximum_bitcast_fusion.qg_in
  5.0 0.5 copy-done
  5.5 0.0 copy-done.1
  5.5 0.0 copy-done.2
  5.5 0.0 copy-done.3
  5.5 65.3 %shard_map.103 = (bf16[4,128,512]{2,1,0:T(8,128)(2,1)S(1)}, bf16[4,128,512]{2,1,0:T(8,128)(2,1)S(1)}) custom-call(bf16[4,128,512]{2,1,0:T(8,128)(2,1)S(1)} %maximum_bitcast_fusion.1.kv_in, bf16[4,128,1024]{2,1,0:T(8,128)(2,1)S(1)} %maximum_bitcast_fusion.qg_in, s32[1,128]{1,0:T(1,128)S(1)} %bitcast.18, s32[1,128]{1,0:T(1,128)S(1)} %bitcast.19, ...), custom_call_target="tpu_custom_call" | custom-call | tf_op jit(solution)/shard_map/pallas_call | solution.py:347
  70.7 0.3 copy.19
  71.0 1.2 %copy.22 = bf16[128,16,128]{2,1,0:T(8,128)(2,1)} copy(bf16[128,16,128]{0,2,1:T(8,128)(2,1)S(1)} %bitcast.21) | data formatting | bytes 1048576
  72.3 0.2 copy.21
  72.4 0.9 %copy.24 = bf16[128,8,128]{2,1,0:T(8,128)(2,1)} copy(bf16[128,8,128]{0,2,1:T(8,128)(2,1)S(1)} %bitcast.24) | data formatting | bytes 524288
  73.3 0.2 copy.20
  73.5 0.9 %copy.23 = bf16[128,8,128]{2,1,0:T(8,128)(2,1)} copy(bf16[128,8,128]{0,2,1:T(8,128)(2,1)S(1)} %bitcast.25) | data formatting | bytes 524288
  (2 shorter events, 0.1 us)
Async XLA Ops:
  0.6 1.4 %copy-start.6 = (bf16[128,8,128]{2,1,0:T(8,128)(2,1)S(1)}, bf16[128,8,128]{2,1,0:T(8,128)(2,1)}, u32[]{:S(2)}) copy-start(bf16[128,8,128]{2,1,0:T(8,128)(2,1)} %param.10) | copy-start | bytes 786436
  2.0 1.0 %copy-start.4 = (bf16[128,16,128]{2,1,0:T(8,128)(2,1)S(1)}, bf16[128,16,128]{2,1,0:T(8,128)(2,1)}, u32[]{:S(2)}) copy-start(bf16[128,16,128]{2,1,0:T(8,128)(2,1)} %param.8) | copy-start | bytes 1572868
  3.0 1.0 %copy-start.5 = (bf16[128,16,128]{2,1,0:T(8,128)(2,1)S(1)}, bf16[128,16,128]{2,1,0:T(8,128)(2,1)}, u32[]{:S(2)}) copy-start(bf16[128,16,128]{2,1,0:T(8,128)(2,1)} %param.11) | copy-start | bytes 1572868
  4.8 0.7 copy-start
  4.8 0.7 copy-start.1
  4.8 0.7 copy-start.2
  4.8 0.7 copy-start.3

commit v4 on v3

--- a/solution.py
+++ b/solution.py
@@ -26,7 +26,7 @@
 
 def kernel(
     n, kv_in, qg_in, seg_ref, live_ref, lab_ref, ro_ref, oq, okv,
-    kvb, qgb, meta, segc, rob, bias, pb, ob, rwb, acc, gqb, b2s, b2r, b1s, b1r, kvs,
+    kvb, qgb, meta, segc, rob, pb, ob, rwb, acc, gqb, b2s, b2r, b1s, b1r, kvs,
     me_in, kvt, sb, dsb, inv,
     ssem, rsem,
 ):
@@ -91,7 +91,7 @@
         send(KV_A, kv_in.at[d], kchunk(8 + r), base + d, d, r)
         send(ME_A, me_in, meta.at[8 + r], base + d, d, r)
     for k in range(R):
-        c = lax.rem(lax.div(r, 2) + k // 2, 2) * 2 + lax.rem(r + k, 2)
+        c = lax.rem(5 - k + 2 * lax.div(r, 2), R)
         wait_recv(KV_A, c, kchunk(8 + c))
         wait_recv(ME_A, c, meta.at[8 + c])
 
@@ -154,32 +154,41 @@
     def forward(step, carry):
         i = R - 1 - step
 
-        @pl.when(has2)
-        def _():
-            wait_recv(KV_2, i, kchunk(i))
-            wait_recv(ME_2, i, meta.at[i])
-
-        seg_column(i)
         seg_q = meta[8 + i, 0:1, :]
-        for j in range(9):
+        q2s = [two(qgb, i, g, 0) for g in range(2)]
+
+        def scores(j, tops):
+            at = slice(j * T, (j + 1) * T)
             ok = segc[rows((i + j) * T)] == seg_q
             if j in (0, 8):
                 kk = lax.broadcasted_iota(jnp.int32, (T, T), 0)
                 tq = lax.broadcasted_iota(jnp.int32, (T, T), 1)
                 ok = jnp.logical_and(ok, kk > tq if j == 0 else kk <= tq)
-            bias[j * T : (j + 1) * T] = jnp.where(ok, 0.0, NEGATIVE)
+            b = jnp.where(ok, 0.0, NEGATIVE)
+            b = jnp.concatenate([b, b], axis=1)
+            new = []
+            for g in range(2):
+                raw = dot(kvb[rows((i + j) * T), g * D : (g + 1) * D], q2s[g], 1, 1)
+                x = raw * (SCALE * LOG2E) + b
+                sb[g, at] = x
+                m = jnp.max(x.reshape(T // 8, 8, 2 * T), axis=0)
+                new.append(jnp.maximum(tops[g], m))
+            return new
+
+        tops = [jnp.full((8, 2 * T), 2 * NEGATIVE, F32)] * 2
+        for j in range(1, 9):
+            tops = scores(j, tops)
+
+        @pl.when(has2)
+        def _():
+            wait_recv(KV_2, i, kchunk(i))
+            wait_recv(ME_2, i, meta.at[i])
+
+        seg_column(i)
+        tops = scores(0, tops)
         total = jnp.zeros((1, T), F32)
         for g in range(2):
-            q2 = two(qgb, i, g, 0)
-            top = None
-            for j in range(9):
-                at = slice(j * T, (j + 1) * T)
-                raw = dot(kvb[rows((i + j) * T), g * D : (g + 1) * D], q2, 1, 1)
-                b = bias[at]
-                x = raw * (SCALE * LOG2E) + jnp.concatenate([b, b], axis=1)
-                sb[g, at] = x
-                m = jnp.max(x.reshape(T // 8, 8, 2 * T), axis=0)
-                top = m if top is None else jnp.maximum(top, m)
+            top = tops[g]
             top = jnp.max(top, axis=0, keepdims=True)
             total_e = None
             for j in range(9):
@@ -214,6 +223,7 @@
         reward = jnp.sum(rwb[:, i, 0:1, :], axis=0)
         live = meta[8 + i, 1:2, :]
         pg = live * (jax.nn.sigmoid(reward) - meta[8 + i, 2:3, :])
+        held = []
         for g in range(2):
             q2 = two(qgb, i, g, 0)
             go = two(qgb, i, g, 4 * D).astype(F32).T
@@ -228,15 +238,30 @@
             part = inv[2 * i + g, 0:1, :]
             delta = jnp.sum(ga_f * ob[2 * i + g], axis=0, keepdims=True) * part
             ga2 = (ga_f * part).T.astype(BF)
-            for j in range(9):
-                at = slice(j * T, (j + 1) * T)
-                here = rows((i + j) * T)
-                low = pb[2 * i + g, at]
-                dp = dot(kvb[here, (2 + g) * D : (3 + g) * D], ga_t, 1, 0)
-                ds = (low.astype(F32) * (dp * part - delta)).astype(BF)
-                dsb[g, at] = ds
-                acc[here, g * D : (g + 1) * D] += dot(ds, q2, 1, 0)
-                acc[here, (2 + g) * D : (3 + g) * D] += dot(low, ga2, 1, 0)
+            held.append((q2, ga_t, part, delta, ga2))
+
+        def terms(g, j):
+            q2, ga_t, part, delta, ga2 = held[g]
+            at = slice(j * T, (j + 1) * T)
+            here = rows((i + j) * T)
+            low = pb[2 * i + g, at]
+            dp = dot(kvb[here, (2 + g) * D : (3 + g) * D], ga_t, 1, 0)
+            ds = (low.astype(F32) * (dp * part - delta)).astype(BF)
+            dsb[g, at] = ds
+            acc[here, g * D : (g + 1) * D] += dot(ds, q2, 1, 0)
+            acc[here, (2 + g) * D : (3 + g) * D] += dot(low, ga2, 1, 0)
+
+        for g in range(2):
+            terms(g, 0)
+
+        @pl.when(has2)
+        def _():
+            b2s[i] = packed(i * T).astype(BF)
+            send(B2, b2s.at[i], b2r.at[i], dn, i, i)
+
+        for g in range(2):
+            for j in range(1, 9):
+                terms(g, j)
             gq = dot(kvt[g * D : (g + 1) * D, win(i)], dsb[g], 1, 0) * SCALE
             gq = gq.T.astype(BF)
             gqb[i, :, 2 * g * D : (2 * g + 1) * D] = gq[:T]
@@ -249,11 +274,6 @@
         @pl.when(i != r)
         def _():
             send(OQ, gqb.at[i], oq.at[r], base + i, i, r)
-
-        @pl.when(has2)
-        def _():
-            b2s[i] = packed(i * T).astype(BF)
-            send(B2, b2s.at[i], b2r.at[i], dn, i, i)
 
         return carry
 
@@ -358,7 +378,6 @@
             vmem((12, 8, T), F32),
             vmem((span, T), F32),
             vmem((4, D, D), F32),
-            vmem((WINDOW + T, T), F32),
             vmem((8, WINDOW + T, 2 * T), BF),
             vmem((8, D, 2 * T), F32),
             vmem((R, R, 8, T), F32),

time: 74.6 us -> 72 us (0.965)
  Pallas kernels: 65.3 us -> 62.5 us
    pallas_call x1, Pallas kernels: 65.3 us -> 62.5 us  [local(): pl.pallas_call(functools.partial(kernel, n), out_shape=[jax.ShapeDtypeStr...]
where the time goes in v4:
time: 72 us; the launch traced here: 71.6 us
  Pallas kernels  62.5 us (87%)
  local copies, waits for them, and re-layouts  8.18 us (11%)
  between operations  0.77 us (1%)
    pallas_call x1, Pallas kernels, local(): pl.pallas_call(functools.partial(kernel, n), out_shape=[jax.ShapeDtypeStr...  62.5 us
    unnamed x21, local copies, waits for them, and re-layouts  6.81 us

profile of v4, /device:TPU:15, one launch (start us, length us, event | category | flops | bytes accessed | tf_op | source)
XLA Modules:
  0.0 71.6 jit_solution(17948454075404673791)
XLA Ops:
  0.6 0.0 copy-start.6
  0.6 1.2 %copy.11 = bf16[128,8,128]{0,2,1:T(8,128)(2,1)S(1)} copy(bf16[128,8,128]{2,1,0:T(8,128)(2,1)} %param.9) | data formatting | bytes 524288 | tf_op args[1]
  1.8 0.1 copy.13
  2.0 0.0 copy-done.6
  2.0 0.0 copy-start.4
  2.0 0.2 copy.12
  2.2 0.1 copy.14
  2.4 0.6 copy-done.4
  3.0 0.0 copy-start.5
  3.0 0.5 copy.15
  3.5 0.2 copy.17
  3.7 0.4 copy-done.5
  4.1 0.5 copy.16
  4.5 0.2 copy.18
  4.8 0.0 copy-start
  4.8 0.0 copy-start.1
  4.8 0.0 copy-start.2
  4.8 0.0 copy-start.3
  4.8 0.1 maximum_bitcast_fusion.qg_in
  5.0 0.5 copy-done
  5.5 0.0 copy-done.1
  5.5 0.0 copy-done.2
  5.5 0.0 copy-done.3
  5.5 62.5 %shard_map.103 = (bf16[4,128,512]{2,1,0:T(8,128)(2,1)S(1)}, bf16[4,128,512]{2,1,0:T(8,128)(2,1)S(1)}) custom-call(bf16[4,128,512]{2,1,0:T(8,128)(2,1)S(1)} %maximum_bitcast_fusion.1.kv_in, bf16[4,128,1024]{2,1,0:T(8,128)(2,1)S(1)} %maximum_bitcast_fusion.qg_in, s32[1,128]{1,0:T(1,128)S(1)} %bitcast.18, s32[1,128]{1,0:T(1,128)S(1)} %bitcast.19, ...), custom_call_target="tpu_custom_call" | custom-call | tf_op jit(solution)/shard_map/pallas_call | solution.py:367
  68.0 0.3 copy.19
  68.2 1.2 %copy.22 = bf16[128,16,128]{2,1,0:T(8,128)(2,1)} copy(bf16[128,16,128]{0,2,1:T(8,128)(2,1)S(1)} %bitcast.21) | data formatting | bytes 1048576
  69.5 0.2 copy.21
  69.7 0.9 %copy.24 = bf16[128,8,128]{2,1,0:T(8,128)(2,1)} copy(bf16[128,8,128]{0,2,1:T(8,128)(2,1)S(1)} %bitcast.24) | data formatting | bytes 524288
  70.5 0.2 copy.20
  70.7 0.9 %copy.23 = bf16[128,8,128]{2,1,0:T(8,128)(2,1)} copy(bf16[128,8,128]{0,2,1:T(8,128)(2,1)S(1)} %bitcast.25) | data formatting | bytes 524288
  (2 shorter events, 0.1 us)
Async XLA Ops:
  0.6 1.4 %copy-start.6 = (bf16[128,8,128]{2,1,0:T(8,128)(2,1)S(1)}, bf16[128,8,128]{2,1,0:T(8,128)(2,1)}, u32[]{:S(2)}) copy-start(bf16[128,8,128]{2,1,0:T(8,128)(2,1)} %param.10) | copy-start | bytes 786436
  2.0 1.0 %copy-start.4 = (bf16[128,16,128]{2,1,0:T(8,128)(2,1)S(1)}, bf16[128,16,128]{2,1,0:T(8,128)(2,1)}, u32[]{:S(2)}) copy-start(bf16[128,16,128]{2,1,0:T(8,128)(2,1)} %param.8) | copy-start | bytes 1572868
  3.0 1.0 %copy-start.5 = (bf16[128,16,128]{2,1,0:T(8,128)(2,1)S(1)}, bf16[128,16,128]{2,1,0:T(8,128)(2,1)}, u32[]{:S(2)}) copy-start(bf16[128,16,128]{2,1,0:T(8,128)(2,1)} %param.11) | copy-start | bytes 1572868
  4.8 0.7 copy-start
  4.8 0.7 copy-start.1
  4.8 0.7 copy-start.2
  4.8 0.7 copy-start.3

commit v5 on v4

--- a/solution.py
+++ b/solution.py
@@ -219,6 +219,20 @@
             [acc[rows(start), : 2 * D] * SCALE, acc[rows(start), 2 * D :]], axis=1
         )
 
+    def near(c):
+        @pl.when(mid)
+        def _():
+            wait_recv(B2, c, b2r.at[c])
+            b1s[c] = (packed((4 + c) * T) + b2r[c].astype(F32)).astype(BF)
+
+        @pl.when(jnp.logical_and(has_dn, jnp.logical_not(has_up)))
+        def _():
+            b1s[c] = packed((4 + c) * T).astype(BF)
+
+        @pl.when(has_dn)
+        def _():
+            send(B1, b1s.at[c], b1r.at[c], dn, c, c)
+
     def backward(i, carry):
         reward = jnp.sum(rwb[:, i, 0:1, :], axis=0)
         live = meta[8 + i, 1:2, :]
@@ -259,9 +273,17 @@
             b2s[i] = packed(i * T).astype(BF)
             send(B2, b2s.at[i], b2r.at[i], dn, i, i)
 
+        for span, ready in ((range(1, 5), (0, 1)), (range(5, 7), (2,)), (range(7, 9), (3,))):
+            for j in span:
+                for g in range(2):
+                    terms(g, j)
+
+            @pl.when(i == R - 1)
+            def _():
+                for c in ready:
+                    near(c)
+
         for g in range(2):
-            for j in range(1, 9):
-                terms(g, j)
             gq = dot(kvt[g * D : (g + 1) * D, win(i)], dsb[g], 1, 0) * SCALE
             gq = gq.T.astype(BF)
             gqb[i, :, 2 * g * D : (2 * g + 1) * D] = gq[:T]
@@ -278,24 +300,6 @@
         return carry
 
     lax.fori_loop(0, R, backward, 0)
-
-    def near(c, carry):
-        @pl.when(mid)
-        def _():
-            wait_recv(B2, c, b2r.at[c])
-            b1s[c] = (packed((4 + c) * T) + b2r[c].astype(F32)).astype(BF)
-
-        @pl.when(jnp.logical_and(has_dn, jnp.logical_not(has_up)))
-        def _():
-            b1s[c] = packed((4 + c) * T).astype(BF)
-
-        @pl.when(has_dn)
-        def _():
-            send(B1, b1s.at[c], b1r.at[c], dn, c, c)
-
-        return carry
-
-    lax.fori_loop(0, R, near, 0)
 
     def own(c, carry):
         @pl.when(has_up)

time: 72 us -> 73.1 us (1.015)
  Pallas kernels: 62.5 us -> 63.7 us
    pallas_call x1, Pallas kernels: 62.5 us -> 63.7 us  [local(): pl.pallas_call(functools.partial(kernel, n), out_shape=[jax.ShapeDtypeStr...]
where the time goes in v5:
time: 73.1 us; the launch traced here: 72.9 us
  Pallas kernels  63.7 us (87%)
  local copies, waits for them, and re-layouts  8.18 us (11%)
  between operations  0.77 us (1%)
    pallas_call x1, Pallas kernels, local(): pl.pallas_call(functools.partial(kernel, n), out_shape=[jax.ShapeDtypeStr...  63.7 us
    unnamed x21, local copies, waits for them, and re-layouts  6.81 us

profile of v5, /device:TPU:15, one launch (start us, length us, event | category | flops | bytes accessed | tf_op | source)
XLA Modules:
  0.0 72.9 jit_solution(6448922810996429912)
XLA Ops:
  0.6 0.0 copy-start.6
  0.6 1.2 %copy.11 = bf16[128,8,128]{0,2,1:T(8,128)(2,1)S(1)} copy(bf16[128,8,128]{2,1,0:T(8,128)(2,1)} %param.9) | data formatting | bytes 524288 | tf_op args[1]
  1.8 0.1 copy.13
  2.0 0.0 copy-done.6
  2.0 0.0 copy-start.4
  2.0 0.2 copy.12
  2.2 0.1 copy.14
  2.4 0.6 copy-done.4
  3.0 0.0 copy-start.5
  3.0 0.5 copy.15
  3.5 0.2 copy.17
  3.7 0.4 copy-done.5
  4.1 0.5 copy.16
  4.5 0.2 copy.18
  4.8 0.0 copy-start
  4.8 0.0 copy-start.1
  4.8 0.0 copy-start.2
  4.8 0.0 copy-start.3
  4.8 0.1 maximum_bitcast_fusion.qg_in
  5.0 0.5 copy-done
  5.5 0.0 copy-done.1
  5.5 0.0 copy-done.2
  5.5 0.0 copy-done.3
  5.5 63.7 %shard_map.103 = (bf16[4,128,512]{2,1,0:T(8,128)(2,1)S(1)}, bf16[4,128,512]{2,1,0:T(8,128)(2,1)S(1)}) custom-call(bf16[4,128,512]{2,1,0:T(8,128)(2,1)S(1)} %maximum_bitcast_fusion.1.kv_in, bf16[4,128,1024]{2,1,0:T(8,128)(2,1)S(1)} %maximum_bitcast_fusion.qg_in, s32[1,128]{1,0:T(1,128)S(1)} %bitcast.18, s32[1,128]{1,0:T(1,128)S(1)} %bitcast.19, ...), custom_call_target="tpu_custom_call" | custom-call | tf_op jit(solution)/shard_map/pallas_call | solution.py:371
  69.2 0.3 copy.19
  69.5 1.2 %copy.22 = bf16[128,16,128]{2,1,0:T(8,128)(2,1)} copy(bf16[128,16,128]{0,2,1:T(8,128)(2,1)S(1)} %bitcast.21) | data formatting | bytes 1048576
  70.7 0.2 copy.21
  70.9 0.9 %copy.24 = bf16[128,8,128]{2,1,0:T(8,128)(2,1)} copy(bf16[128,8,128]{0,2,1:T(8,128)(2,1)S(1)} %bitcast.24) | data formatting | bytes 524288
  71.8 0.2 copy.20
  72.0 0.9 %copy.23 = bf16[128,8,128]{2,1,0:T(8,128)(2,1)} copy(bf16[128,8,128]{0,2,1:T(8,128)(2,1)S(1)} %bitcast.25) | data formatting | bytes 524288
  (2 shorter events, 0.1 us)
Async XLA Ops:
  0.6 1.4 %copy-start.6 = (bf16[128,8,128]{2,1,0:T(8,128)(2,1)S(1)}, bf16[128,8,128]{2,1,0:T(8,128)(2,1)}, u32[]{:S(2)}) copy-start(bf16[128,8,128]{2,1,0:T(8,128)(2,1)} %param.10) | copy-start | bytes 786436
  2.0 1.0 %copy-start.4 = (bf16[128,16,128]{2,1,0:T(8,128)(2,1)S(1)}, bf16[128,16,128]{2,1,0:T(8,128)(2,1)}, u32[]{:S(2)}) copy-start(bf16[128,16,128]{2,1,0:T(8,128)(2,1)} %param.8) | copy-start | bytes 1572868
  3.0 1.0 %copy-start.5 = (bf16[128,16,128]{2,1,0:T(8,128)(2,1)S(1)}, bf16[128,16,128]{2,1,0:T(8,128)(2,1)}, u32[]{:S(2)}) copy-start(bf16[128,16,128]{2,1,0:T(8,128)(2,1)} %param.11) | copy-start | bytes 1572868
  4.8 0.7 copy-start
  4.8 0.7 copy-start.1
  4.8 0.7 copy-start.2
  4.8 0.7 copy-start.3

commit v6 on v4

--- a/solution.py
+++ b/solution.py
@@ -178,6 +178,18 @@
         tops = [jnp.full((8, 2 * T), 2 * NEGATIVE, F32)] * 2
         for j in range(1, 9):
             tops = scores(j, tops)
+        rest = []
+        for g in range(2):
+            top = jnp.max(tops[g], axis=0, keepdims=True)
+            total_e = jnp.zeros((8, 2 * T), F32)
+            for j in range(1, 9):
+                at = slice(j * T, (j + 1) * T)
+                e = jnp.exp2(sb[g, at] - top)
+                pb[2 * i + g, at] = e.astype(BF)
+                total_e = total_e + jnp.sum(e.reshape(T // 8, 8, 2 * T), axis=0)
+            vt = kvt[(2 + g) * D : (3 + g) * D, pl.ds(pl.multiple_of((i + 1) * T, T), WINDOW)]
+            o = dot(vt, pb[2 * i + g, T:], 1, 0)
+            rest.append((top, jnp.sum(total_e, axis=0, keepdims=True), o))
 
         @pl.when(has2)
         def _():
@@ -188,19 +200,18 @@
         tops = scores(0, tops)
         total = jnp.zeros((1, T), F32)
         for g in range(2):
-            top = tops[g]
-            top = jnp.max(top, axis=0, keepdims=True)
-            total_e = None
-            for j in range(9):
-                at = slice(j * T, (j + 1) * T)
-                e = jnp.exp2(sb[g, at] - top)
-                pb[2 * i + g, at] = e.astype(BF)
-                m = jnp.sum(e.reshape(T // 8, 8, 2 * T), axis=0)
-                total_e = m if total_e is None else total_e + m
-            part = 1.0 / jnp.sum(total_e, axis=0, keepdims=True)
+            old, old_sum, old_o = rest[g]
+            top = jnp.max(tops[g], axis=0, keepdims=True)
+            shrink = jnp.exp2(old - top)
+            e = jnp.exp2(sb[g, :T] - top)
+            low = e.astype(BF)
+            pb[2 * i + g, :T] = low
+            far = 1.0 / (old_sum * shrink + jnp.sum(e, axis=0, keepdims=True))
+            part = far * shrink
             inv[2 * i + g] = jnp.broadcast_to(part, (8, 2 * T))
-            vt = kvt[(2 + g) * D : (3 + g) * D, win(i)]
-            o = dot(vt, pb[2 * i + g], 1, 0) * part
+            inv[8 + 2 * i + g] = jnp.broadcast_to(far, (8, 2 * T))
+            vt = kvt[(2 + g) * D : (3 + g) * D, rows(i * T)]
+            o = old_o * part + dot(vt, low, 1, 0) * far
             ob[2 * i + g] = o
             w = o[:, :T] * rob[2 * g] + o[:, T:] * rob[2 * g + 1]
             total = total + jnp.sum(w, axis=0, keepdims=True)
@@ -236,17 +247,20 @@
             ).astype(BF)
             ga_f = ga_t.astype(F32)
             part = inv[2 * i + g, 0:1, :]
-            delta = jnp.sum(ga_f * ob[2 * i + g], axis=0, keepdims=True) * part
+            far = inv[8 + 2 * i + g, 0:1, :]
+            delta = jnp.sum(ga_f * ob[2 * i + g], axis=0, keepdims=True)
             ga2 = (ga_f * part).T.astype(BF)
-            held.append((q2, ga_t, part, delta, ga2))
+            ga0 = (ga_f * far).T.astype(BF)
+            held.append((q2, ga_t, (far, part), delta, (ga0, ga2)))
 
         def terms(g, j):
-            q2, ga_t, part, delta, ga2 = held[g]
+            q2, ga_t, parts, delta, gas = held[g]
+            part, ga2 = parts[min(j, 1)], gas[min(j, 1)]
             at = slice(j * T, (j + 1) * T)
             here = rows((i + j) * T)
             low = pb[2 * i + g, at]
             dp = dot(kvb[here, (2 + g) * D : (3 + g) * D], ga_t, 1, 0)
-            ds = (low.astype(F32) * (dp * part - delta)).astype(BF)
+            ds = (low.astype(F32) * ((dp - delta) * part)).astype(BF)
             dsb[g, at] = ds
             acc[here, g * D : (g + 1) * D] += dot(ds, q2, 1, 0)
             acc[here, (2 + g) * D : (3 + g) * D] += dot(low, ga2, 1, 0)
@@ -392,7 +406,7 @@
             vmem((4 * D, span), BF),
             vmem((2, WINDOW + T, 2 * T), F32),
             vmem((2, WINDOW + T, 2 * T), BF),
-            vmem((8, 8, 2 * T), F32),
+            vmem((16, 8, 2 * T), F32),
             pltpu.SemaphoreType.DMA((12, R)),
             pltpu.SemaphoreType.DMA((12, R)),
         ],

time: 72 us -> 72.5 us (level)
  no operation moved by 1% of the time
where the time goes in v6:
time: 72.5 us; the launch traced here: 72.1 us
  Pallas kernels  63 us (87%)
  local copies, waits for them, and re-layouts  8.18 us (11%)
  between operations  0.77 us (1%)
    pallas_call x1, Pallas kernels, local(): pl.pallas_call(functools.partial(kernel, n), out_shape=[jax.ShapeDtypeStr...  63 us
    unnamed x21, local copies, waits for them, and re-layouts  6.81 us

profile of v6, /device:TPU:15, one launch (start us, length us, event | category | flops | bytes accessed | tf_op | source)
XLA Modules:
  0.0 72.1 jit_solution(17687847041777603932)
XLA Ops:
  0.6 0.0 copy-start.6
  0.6 1.2 %copy.11 = bf16[128,8,128]{0,2,1:T(8,128)(2,1)S(1)} copy(bf16[128,8,128]{2,1,0:T(8,128)(2,1)} %param.9) | data formatting | bytes 524288 | tf_op args[1]
  1.8 0.1 copy.13
  2.0 0.0 copy-done.6
  2.0 0.0 copy-start.4
  2.0 0.2 copy.12
  2.2 0.1 copy.14
  2.4 0.6 copy-done.4
  3.0 0.0 copy-start.5
  3.0 0.5 copy.15
  3.5 0.2 copy.17
  3.7 0.4 copy-done.5
  4.1 0.5 copy.16
  4.5 0.2 copy.18
  4.8 0.0 copy-start
  4.8 0.0 copy-start.1
  4.8 0.0 copy-start.2
  4.8 0.0 copy-start.3
  4.8 0.1 maximum_bitcast_fusion.qg_in
  5.0 0.5 copy-done
  5.5 0.0 copy-done.1
  5.5 0.0 copy-done.2
  5.5 0.0 copy-done.3
  5.5 63.0 %shard_map.103 = (bf16[4,128,512]{2,1,0:T(8,128)(2,1)S(1)}, bf16[4,128,512]{2,1,0:T(8,128)(2,1)S(1)}) custom-call(bf16[4,128,512]{2,1,0:T(8,128)(2,1)S(1)} %maximum_bitcast_fusion.1.kv_in, bf16[4,128,1024]{2,1,0:T(8,128)(2,1)S(1)} %maximum_bitcast_fusion.qg_in, s32[1,128]{1,0:T(1,128)S(1)} %bitcast.18, s32[1,128]{1,0:T(1,128)S(1)} %bitcast.19, ...), custom_call_target="tpu_custom_call" | custom-call | tf_op jit(solution)/shard_map/pallas_call | solution.py:381
  68.5 0.3 copy.19
  68.8 1.2 %copy.22 = bf16[128,16,128]{2,1,0:T(8,128)(2,1)} copy(bf16[128,16,128]{0,2,1:T(8,128)(2,1)S(1)} %bitcast.21) | data formatting | bytes 1048576
  70.0 0.2 copy.21
  70.2 0.9 %copy.24 = bf16[128,8,128]{2,1,0:T(8,128)(2,1)} copy(bf16[128,8,128]{0,2,1:T(8,128)(2,1)S(1)} %bitcast.24) | data formatting | bytes 524288
  71.1 0.2 copy.20
  71.2 0.9 %copy.23 = bf16[128,8,128]{2,1,0:T(8,128)(2,1)} copy(bf16[128,8,128]{0,2,1:T(8,128)(2,1)S(1)} %bitcast.25) | data formatting | bytes 524288
  (2 shorter events, 0.1 us)
Async XLA Ops:
  0.6 1.4 %copy-start.6 = (bf16[128,8,128]{2,1,0:T(8,128)(2,1)S(1)}, bf16[128,8,128]{2,1,0:T(8,128)(2,1)}, u32[]{:S(2)}) copy-start(bf16[128,8,128]{2,1,0:T(8,128)(2,1)} %param.10) | copy-start | bytes 786436
  2.0 1.0 %copy-start.4 = (bf16[128,16,128]{2,1,0:T(8,128)(2,1)S(1)}, bf16[128,16,128]{2,1,0:T(8,128)(2,1)}, u32[]{:S(2)}) copy-start(bf16[128,16,128]{2,1,0:T(8,128)(2,1)} %param.8) | copy-start | bytes 1572868
  3.0 1.0 %copy-start.5 = (bf16[128,16,128]{2,1,0:T(8,128)(2,1)S(1)}, bf16[128,16,128]{2,1,0:T(8,128)(2,1)}, u32[]{:S(2)}) copy-start(bf16[128,16,128]{2,1,0:T(8,128)(2,1)} %param.11) | copy-start | bytes 1572868
  4.8 0.7 copy-start
  4.8 0.7 copy-start.1
  4.8 0.7 copy-start.2
  4.8 0.7 copy-start.3
